TPU v7x, 256 devices: a whole 4x4x8 slice. The times are simulated.
256 devices in a mesh: sec: 64 (over z, y, core), tile: 4 (over x).
Axes of the slice: x: 4, y: 4, z: 8, core: 2. Of those that a mesh axis runs over, the one named last changes fastest.
Arguments:
- patches: bfloat16 [384, 8, 8, 128, 128], P('sec', 'tile'), may hold values from -6 to 6
- pair_flags: int32 [384, 3], P('sec'), may hold values 0 or 1
- nodes: float32 [2, 384, 8, 8], P(None, 'sec', 'tile'), may hold values from -6 to 6
Outputs:
- relaxed: float32 [2, 384, 8, 8], P(None, 'sec', 'tile')
- measured: float32 [2, 384, 3, 8, 8], P(None, 'sec', None, 'tile')
Inputs may be any that keep to these rules, and one draw needn't show every extreme that they name: `pair_flags`: flags of pairs whose partner lies past the last section are ignored.
All inputs are finite; a program needn't handle non-finite values. No bound on the sum of `pair_flags` on one device may be relied on, other than what follows from the above.
Results may differ from a plain program's by a relative error of at most 0.0081.
Values may be sent and summed in bfloat16 or wider, within the bound.
No kernel may reach another device: no remote copies, remote signals or barrier semaphores. Data moves between devices by JAX's collectives and lax.ppermute only.
A program may use at most 128 MiB of HBM per device.

v0:
```python
import math

import jax
import jax.numpy as jnp
from jax import lax
from jax.sharding import PartitionSpec as P

SWEEPS = 8


STEP_SIZE = 0.08
EPSILON = 1e-06


def shifted(value, axis, by):
    count = lax.axis_size(axis)
    pairs = [(i, i + by) for i in range(count) if 0 <= i + by < count]
    return lax.ppermute(value, axis, pairs)


def in_order(tiles, dim):
    lengths = list(tiles.shape[1:])
    lengths[dim] *= tiles.shape[0]
    return jnp.moveaxis(tiles, 0, dim).reshape(lengths)


def copy_for_each(value, axis):
    count = lax.axis_size(axis)
    return lax.all_to_all(
        jnp.broadcast_to(value[None], (count, *value.shape)), axis, 0, 0, tiled=True
    )


def collect(value, axis, dim):
    return in_order(copy_for_each(value, axis), dim)


def padded(block, sides, width):
    for axis, dim in sides:
        count = lax.axis_size(axis)
        forward = [(i, i + 1) for i in range(count - 1)]
        backward = [(target, source) for source, target in forward]
        low = lax.ppermute(
            lax.slice_in_dim(block, block.shape[dim] - width, None, axis=dim), axis, forward
        )
        high = lax.ppermute(lax.slice_in_dim(block, 0, width, axis=dim), axis, backward)
        block = jnp.concatenate([low, block, high], axis=dim)
    return block


def transform_tables(length):
    index = jnp.arange(length, dtype=jnp.int32)
    phase = (index[:, None] * index[None, :] % length).astype(jnp.float32) * (
        2.0 * math.pi / length
    )
    cosine = jnp.cos(phase)
    sine = jnp.sin(phase)
    forward_first = jnp.concatenate([cosine, sine], axis=1).astype(jnp.bfloat16)
    forward_second = jnp.stack(
        [jnp.stack([cosine, -sine], 1), jnp.stack([-sine, -cosine], 1)], 0
    ).astype(jnp.bfloat16)
    inverse_first = jnp.stack(
        [jnp.stack([cosine, sine], 1), jnp.stack([-sine, cosine], 1)], 0
    ).astype(jnp.bfloat16)
    inverse_second = jnp.stack([cosine, -sine], 1).astype(jnp.bfloat16)
    shifts = jnp.where(index < length // 2, index, index - length).astype(jnp.float32)
    return (forward_first, forward_second, inverse_first, inverse_second, shifts)


def spectrum(block, tabs):
    length = block.shape[-1]
    half = jnp.einsum("...aj,jm->...am", block, tabs[0], preferred_element_type=jnp.float32).astype(
        jnp.bfloat16
    )
    half = half.reshape(half.shape[:-1] + (2, length))
    return jnp.einsum(
        "rahj,...jhk->...rak", tabs[1], half, preferred_element_type=jnp.float32
    ).astype(jnp.bfloat16)


def measure(first_spec, second_spec, weight, tabs):
    length = first_spec.shape[-1]
    left = first_spec.astype(jnp.float32)
    right = second_spec.astype(jnp.float32)
    real = left[..., 0, :, :] * right[..., 0, :, :] + left[..., 1, :, :] * right[..., 1, :, :]
    imag = left[..., 0, :, :] * right[..., 1, :, :] - left[..., 1, :, :] * right[..., 0, :, :]
    cross = jnp.stack([real, imag], axis=-3).astype(jnp.bfloat16)
    back = jnp.einsum(
        "...qaj,qjrk->...rak", cross, tabs[2], preferred_element_type=jnp.float32
    ).astype(jnp.bfloat16)
    corr = jnp.einsum("arj,...rjk->...ak", tabs[3], back, preferred_element_type=jnp.float32) * (
        1.0 / float(length) ** 3
    )
    power = corr * corr
    total = jnp.mean(power, axis=(-2, -1)) + EPSILON
    along_rows = jnp.mean(power * tabs[4][:, None], axis=(-2, -1))
    along_cols = jnp.mean(power * tabs[4][None, :], axis=(-2, -1))
    return jnp.stack([along_rows / total, along_cols / total], 0) * weight


def grid_force(u):
    rows = u.shape[2]
    cols = u.shape[3]
    row_place = jnp.arange(rows, dtype=jnp.int32)
    col_place = jnp.arange(cols, dtype=jnp.int32)
    has_up = (row_place > 0).astype(jnp.float32)[:, None]
    has_down = (row_place < rows - 1).astype(jnp.float32)[:, None]
    has_left = (col_place > 0).astype(jnp.float32)[None, :]
    has_right = (col_place < cols - 1).astype(jnp.float32)[None, :]
    zero_row = jnp.zeros_like(u[:, :, :1])
    zero_col = jnp.zeros_like(u[..., :1])
    above = jnp.concatenate([zero_row, u[:, :, :-1]], axis=2)
    below = jnp.concatenate([u[:, :, 1:], zero_row], axis=2)
    left = jnp.concatenate([zero_col, u[..., :-1]], axis=3)
    right = jnp.concatenate([u[..., 1:], zero_col], axis=3)
    return (
        has_up * (above - u)
        + has_down * (below - u)
        + has_left * (left - u)
        + has_right * (right - u)
    )


def shards(patches, pair_flags, nodes):
    tabs = transform_tables(patches.shape[-1])
    local = patches.shape[0]
    reach = pair_flags.shape[1]
    own = spectrum(patches, tabs)
    received = shifted(patches[:reach], "sec", -1)
    ahead = spectrum(received, tabs)
    extended = jnp.concatenate([own, ahead], axis=0)
    sections = lax.axis_size("sec") * local
    placed = lax.axis_index("sec") * local + jnp.arange(local, dtype=jnp.int32)
    offsets = jnp.arange(1, reach + 1, dtype=jnp.int32)
    weights = pair_flags.astype(jnp.float32) * (
        placed[:, None] + offsets[None, :] < sections
    ).astype(jnp.float32)

    def one_section(items):
        mine, other, weight = items
        return measure(mine, other, weight, tabs)

    columns = []
    for step in range(reach):
        values = lax.map(
            one_section, (own, extended[step + 1 : step + 1 + local], weights[:, step])
        )
        columns.append(jnp.transpose(values, (1, 0, 2, 3)))
    measured = jnp.stack(columns, axis=2)
    rows_local = nodes.shape[2]
    node_full = collect(nodes, "tile", 2)
    pair_full = collect(measured, "tile", 3)
    spread_full = jnp.broadcast_to(weights[None, :, :, None, None], (1,) + pair_full.shape[1:])
    stacked_full = jnp.concatenate([pair_full, spread_full], axis=0)
    earlier_full = shifted(stacked_full[:, local - reach :], "sec", 1)
    terms_full = jnp.concatenate([earlier_full, stacked_full], axis=1)
    state = node_full
    for sweep in range(SWEEPS):
        window = padded(state, (("sec", 1),), reach)
        spring = jnp.zeros_like(state)
        for step in range(reach):
            offset = step + 1
            resid = terms_full[2:3, :, step] * (
                window[:, offset : offset + local + reach]
                - window[:, : local + reach]
                - terms_full[:2, :, step]
            )
            spring = spring + resid[:, reach:] - resid[:, reach - offset : reach - offset + local]
        state = state + STEP_SIZE * (grid_force(state) + spring)
    positions = lax.dynamic_slice_in_dim(state, lax.axis_index("tile") * rows_local, rows_local, 2)
    return (positions, measured)


def solution(mesh):
    placed = (P("sec", "tile", None, None, None), P("sec", None), P(None, "sec", "tile", None))
    return jax.shard_map(
        shards,
        mesh=mesh,
        in_specs=placed,
        out_specs=(P(None, "sec", "tile", None), P(None, "sec", None, "tile", None)),
        check_vma=False,
    )
```

profile of v0, /device:TPU:121, one launch (start us, length us, event | category | flops | bytes accessed | tf_op | source)
XLA Modules:
  0.0 266.6 jit_solution(10343909609739596602)
XLA Ops:
  0.6 2.9 %slice.520 = bf16[3,2,8,128,128]{4,3,2,1,0:T(8,128)(2,1)} slice(bf16[6,2,8,128,128]{4,3,2,1,0:T(8,128)(2,1)} %param.9), slice={[0:3], [0:2], [0:8], [0:128], [0:128]} | slice | bytes 3145728 | tf_op jit(solution)/shard_map/slice | solution.py:129
  3.5 2.6 collective-permute-start
  7.5 4.0 %all-to-all-start = ((f32[4,1,192]{2,1,0:T(1,128)}), f32[4,1,192]{2,1,0:T(1,128)S(1)}, u32[]{:S(2)}, u32[]{:S(2)}) async-start(f32[4,1,192]{2,1,0:T(1,128)} %reshape.454), calls=%async_computation | async-start | bytes 8192 | tf_op jit(solution)/shard_map/all_to_all | solution.py:29
  12.7 1.8 convolution_convert_fusion
  14.7 3.8 %fusion.68 = bf16[6,2,8,2,128,128]{4,5,3,2,1,0:T(8,128)(2,1)} fusion(bf16[6,2,8,128,2,128,1]{3,5,4,6,2,1,0:T(8,128)(2,1)S(1)} %bitcast.400, bf16[1,128,2,128]{3,1,2,0:T(8,128)(2,1)S(1)} %get-tuple-element.470, bf16[1,128,2,128]{3,1,2,0:T(8,128)(2,1)S(1)} %fusion.199), kind=kOutput, calls=%fused_computation.100 | convolution fusion | flops 1614020608 | bytes 12713984 | tf_op jit(solution)/shard_map/rahj,...jhk->...rak/dot_general | solution.py:76
  18.5 8.7 %copy.35 = bf16[6,2,8,2,128,128]{5,4,3,2,1,0:T(8,128)(2,1)} copy(bf16[6,2,8,2,128,128]{4,5,3,2,1,0:T(8,128)(2,1)} %fusion.68) | data formatting | bytes 12582912
  28.5 6.6 %collective-permute-start.2 = (f32[2,3,8,8]{3,2,1,0:T(8,128)S(1)}, f32[2,3,8,8]{3,2,1,0:T(8,128)S(1)}, u32[]{:S(2)}, u32[]{:S(2)}) collective-permute-start(f32[2,3,8,8]{3,2,1,0:T(8,128)S(1)} %get-tuple-element.466), channel_id=1, source_target_pairs={{0,4},{4,8},{8,12},{12,16},{16,20},{20,24},{24,28},{28,32},{32,36}... | collective-permute-start | bytes 4616 | tf_op jit(solution)/shard_map/ppermute | solution.py:43
  35.1 2.1 collective-permute-start.3
  37.3 2.4 convolution_convert_fusion.1
  40.8 1.8 copy-done
  42.5 6.8 %fusion.67 = (bf16[6,2,8,2,128,128]{4,5,3,2,1,0:T(8,128)(2,1)}, bf16[6,2,8,2,128,128]{4,5,3,2,1,0:T(8,128)(2,1)}, bf16[6,2,8,2,128,128]{4,5,3,2,1,0:T(8,128)(2,1)}) fusion(bf16[6,2,8,2,128,128]{4,5,3,2,1,0:T(8,128)(2,1)S(1)} %copy-done, bf16[3,2,8,2,128,128]{4,5,3,2,1,0:T(8,128)(2,1)S(1)} %fusion.69), kind=kLoop, calls=%fused_computation.99 | loop fusion | flops 9437184 | bytes 28311552 | tf_op jit(solution)/shard_map/concatenate | solution.py:131
  49.3 38.5 %while.36 = (s32[]{:T(128)}, f32[6,2,2,8]{3,2,0,1:T(2,128)S(1)}, bf16[6,2,8,2,128,128]{5,4,3,2,1,0:T(8,128)(2,1)}, bf16[6,2,8,2,128,128]{4,5,3,2,1,0:T(8,128)(2,...) while((s32[]{:T(128)}, f32[6,2,2,8]{3,2,0,1:T(2,128)S(1)}, ...), condition=%wide.region_4.5_spmd.clone.clone, body=%wide.region_0.4_spmd.clone.clone.sunk | while | flops 410256032 | bytes 16979568 | solution.py:145
  51.3 1.7 bitcast_convert_fusion.14
  57.7 1.7 bitcast_convert_fusion.14
  64.2 1.7 bitcast_convert_fusion.14
  70.6 1.7 bitcast_convert_fusion.14
  75.0 1.3 constant_dynamic-slice_fusion.6
  77.0 1.7 bitcast_convert_fusion.14
  83.4 1.7 bitcast_convert_fusion.14
  87.9 38.5 %while.37 = (s32[]{:T(128)}, f32[6,2,2,8]{3,2,0,1:T(2,128)S(1)}, bf16[6,2,8,2,128,128]{5,4,3,2,1,0:T(8,128)(2,1)}, bf16[6,2,8,2,128,128]{4,5,3,2,1,0:T(8,128)(2,...) while((s32[]{:T(128)}, f32[6,2,2,8]{3,2,0,1:T(2,128)S(1)}, ...), condition=%wide.region_9.10_spmd.clone.clone, body=%wide.region_5.9_spmd.clone.clone.sunk | while | flops 410256032 | bytes 16979568 | solution.py:145
  87.9 1.3 constant_dynamic-slice_fusion.7
  89.9 1.7 bitcast_convert_fusion.15
  94.3 1.3 constant_dynamic-slice_fusion.7
  96.3 1.7 bitcast_convert_fusion.15
  102.7 1.7 bitcast_convert_fusion.15
  107.2 1.3 constant_dynamic-slice_fusion.7
  109.2 1.7 bitcast_convert_fusion.15
  115.6 1.7 bitcast_convert_fusion.15
  120.0 1.3 constant_dynamic-slice_fusion.7
  122.0 1.7 bitcast_convert_fusion.15
  126.5 38.5 %while.38 = (s32[]{:T(128)}, f32[6,2,2,8]{3,2,0,1:T(2,128)S(1)}, bf16[6,2,8,2,128,128]{5,4,3,2,1,0:T(8,128)(2,1)}, bf16[6,2,8,2,128,128]{4,5,3,2,1,0:T(8,128)(2,...) while((s32[]{:T(128)}, f32[6,2,2,8]{3,2,0,1:T(2,128)S(1)}, ...), condition=%wide.region_14.15_spmd.clone.clone, body=%wide.region_10.14_spmd.clone.clone.sunk | while | flops 410256032 | bytes 16979568 | solution.py:145
  126.5 1.3 constant_dynamic-slice_fusion.8
  128.4 1.7 bitcast_convert_fusion.16
  132.9 1.3 constant_dynamic-slice_fusion.8
  134.9 1.7 bitcast_convert_fusion.16
  141.3 1.7 bitcast_convert_fusion.16
  145.7 1.3 constant_dynamic-slice_fusion.8
  147.7 1.7 bitcast_convert_fusion.16
  154.1 1.7 bitcast_convert_fusion.16
  160.6 1.7 bitcast_convert_fusion.16
  165.9 4.5 %all-to-all-start.1 = ((f32[4,1,576]{2,1,0:T(1,128)}), f32[4,1,576]{2,1,0:T(1,128)S(1)}, u32[]{:S(2)}, u32[]{:S(2)}) async-start(f32[4,1,576]{2,1,0:T(1,128)} %reshape.452), calls=%async_computation.1 | async-start | bytes 20480 | tf_op jit(solution)/shard_map/all_to_all | solution.py:29
  170.4 4.2 %all-to-all-done.1 = f32[4,1,576]{2,1,0:T(1,128)S(1)} async-done(((f32[4,1,576]{2,1,0:T(1,128)}), f32[4,1,576]{2,1,0:T(1,128)S(1)}, u32[]{:S(2)}, u32[]{:S(2)}) %all-to-all-start.1) | async-done | bytes 9248 | tf_op jit(solution)/shard_map/all_to_all | solution.py:29
  175.7 8.4 %collective-permute-start.1 = (f32[3,3,3,8,8]{4,3,1,0,2:T(8,128)S(1)}, f32[3,3,3,8,8]{4,3,1,0,2:T(8,128)S(1)}, u32[]{:S(2)}, u32[]{:S(2)}) collective-permute-start(f32[3,3,3,8,8]{4,3,1,0,2:T(8,128)S(1)} %pad_maximum_fusion.2), channel_id=1, source_target_pairs={{0,4},{4,8},{8,12},{12,16},{16,20},{20,24},{24,28},{28,32},{32,36}... | collective-permute-start | bytes 20744 | tf_op jit(solution)/shard_map/ppermute | solution.py:18
  186.1 7.6 %collective-permute-start.4 = (f32[2,3,8,8]{3,2,1,0:T(8,128)S(1)}, f32[2,3,8,8]{3,2,1,0:T(8,128)S(1)}, u32[]{:S(2)}, u32[]{:S(2)}) collective-permute-start(f32[2,3,8,8]{3,2,1,0:T(8,128)S(1)} %get-tuple-element.460), channel_id=1, source_target_pairs={{0,4},{4,8},{8,12},{12,16},{16,20},{20,24},{24,28},{28,32},{32,36}... | collective-permute-start | bytes 4616 | tf_op jit(solution)/shard_map/ppermute | solution.py:43
  193.7 1.9 collective-permute-start.5
  195.7 6.5 %collective-permute-done.5 = f32[2,3,8,8]{3,2,1,0:T(8,128)S(1)} collective-permute-done((f32[2,3,8,8]{3,2,1,0:T(8,128)S(1)}, f32[2,3,8,8]{3,2,1,0:T(8,128)S(1)}, u32[]{:S(2)}, u32[]{:S(2)}) %collective-permute-start.5) | collective-permute-done | bytes 1568 | tf_op jit(solution)/shard_map/ppermute | solution.py:46
  202.4 1.9 collective-permute-start.6
  204.3 2.4 collective-permute-start.7
  206.8 6.0 %collective-permute-done.7 = f32[2,3,8,8]{3,2,1,0:T(8,128)S(1)} collective-permute-done((f32[2,3,8,8]{3,2,1,0:T(8,128)S(1)}, f32[2,3,8,8]{3,2,1,0:T(8,128)S(1)}, u32[]{:S(2)}, u32[]{:S(2)}) %collective-permute-start.7) | collective-permute-done | bytes 1568 | tf_op jit(solution)/shard_map/ppermute | solution.py:46
  213.0 1.9 collective-permute-start.8
  214.9 2.4 collective-permute-start.9
  217.4 6.0 %collective-permute-done.9 = f32[2,3,8,8]{3,2,1,0:T(8,128)S(1)} collective-permute-done((f32[2,3,8,8]{3,2,1,0:T(8,128)S(1)}, f32[2,3,8,8]{3,2,1,0:T(8,128)S(1)}, u32[]{:S(2)}, u32[]{:S(2)}) %collective-permute-start.9) | collective-permute-done | bytes 1568 | tf_op jit(solution)/shard_map/ppermute | solution.py:46
  223.6 1.9 collective-permute-start.10
  225.5 2.4 collective-permute-start.11
  228.0 6.0 %collective-permute-done.11 = f32[2,3,8,8]{3,2,1,0:T(8,128)S(1)} collective-permute-done((f32[2,3,8,8]{3,2,1,0:T(8,128)S(1)}, f32[2,3,8,8]{3,2,1,0:T(8,128)S(1)}, u32[]{:S(2)}, u32[]{:S(2)}) %collective-permute-start.11) | collective-permute-done | bytes 1568 | tf_op jit(solution)/shard_map/ppermute | solution.py:46
  234.2 1.9 collective-permute-start.12
  236.1 2.4 collective-permute-start.13
  238.6 6.0 %collective-permute-done.13 = f32[2,3,8,8]{3,2,1,0:T(8,128)S(1)} collective-permute-done((f32[2,3,8,8]{3,2,1,0:T(8,128)S(1)}, f32[2,3,8,8]{3,2,1,0:T(8,128)S(1)}, u32[]{:S(2)}, u32[]{:S(2)}) %collective-permute-start.13) | collective-permute-done | bytes 1568 | tf_op jit(solution)/shard_map/ppermute | solution.py:46
  244.8 1.9 collective-permute-start.14
  246.7 2.4 collective-permute-start.15
  249.2 6.0 %collective-permute-done.15 = f32[2,3,8,8]{3,2,1,0:T(8,128)S(1)} collective-permute-done((f32[2,3,8,8]{3,2,1,0:T(8,128)S(1)}, f32[2,3,8,8]{3,2,1,0:T(8,128)S(1)}, u32[]{:S(2)}, u32[]{:S(2)}) %collective-permute-start.15) | collective-permute-done | bytes 1568 | tf_op jit(solution)/shard_map/ppermute | solution.py:46
  255.4 1.9 collective-permute-start.16
  257.3 2.4 collective-permute-start.17
  259.9 6.0 %collective-permute-done.17 = f32[2,3,8,8]{3,2,1,0:T(8,128)S(1)} collective-permute-done((f32[2,3,8,8]{3,2,1,0:T(8,128)S(1)}, f32[2,3,8,8]{3,2,1,0:T(8,128)S(1)}, u32[]{:S(2)}, u32[]{:S(2)}) %collective-permute-start.17) | collective-permute-done | bytes 1568 | tf_op jit(solution)/shard_map/ppermute | solution.py:46
  (240 shorter events, 84.5 us)
Async XLA Ops:
  0.6 12.1 %copy-start.1 = (bf16[6,2,8,128,128]{4,3,2,1,0:T(8,128)(2,1)S(1)}, bf16[6,2,8,128,128]{4,3,2,1,0:T(8,128)(2,1)}, u32[]{:S(2)}) copy-start(bf16[6,2,8,128,128]{4,3,2,1,0:T(8,128)(2,1)} %param.9) | copy-start | bytes 9437188
  3.5 33.8 %collective-permute-start = (bf16[3,2,8,128,128]{4,3,2,1,0:T(8,128)(2,1)}, bf16[3,2,8,128,128]{4,3,2,1,0:T(8,128)(2,1)}, u32[]{:S(2)}, u32[]{:S(2)}) collective-permute-start(bf16[3,2,8,128,128]{4,3,2,1,0:T(8,128)(2,1)} %slice.520), channel_id=1, source_target_pairs={{4,0},{8,4},{12,8},{16,12},{20,16},{24,20},{28,24},{32,28},{36,32}... | collective-permute-start | bytes 4718600 | tf_op jit(solution)/shard_map/ppermute | solution.py:18
  7.5 19.7 %all-to-all-start = ((f32[4,1,192]{2,1,0:T(1,128)}), f32[4,1,192]{2,1,0:T(1,128)S(1)}, u32[]{:S(2)}, u32[]{:S(2)}) async-start(f32[4,1,192]{2,1,0:T(1,128)} %reshape.454), calls=%async_computation | async-start | bytes 8192 | tf_op jit(solution)/shard_map/all_to_all | solution.py:29
  12.7 1.9 copy-start.2
  28.5 141.9 %collective-permute-start.2 = (f32[2,3,8,8]{3,2,1,0:T(8,128)S(1)}, f32[2,3,8,8]{3,2,1,0:T(8,128)S(1)}, u32[]{:S(2)}, u32[]{:S(2)}) collective-permute-start(f32[2,3,8,8]{3,2,1,0:T(8,128)S(1)} %get-tuple-element.466), channel_id=1, source_target_pairs={{0,4},{4,8},{8,12},{12,16},{16,20},{20,24},{24,28},{28,32},{32,36}... | collective-permute-start | bytes 4616 | tf_op jit(solution)/shard_map/ppermute | solution.py:43
  35.1 135.3 %collective-permute-start.3 = (f32[2,3,8,8]{3,2,1,0:T(8,128)S(1)}, f32[2,3,8,8]{3,2,1,0:T(8,128)S(1)}, u32[]{:S(2)}, u32[]{:S(2)}) collective-permute-start(f32[2,3,8,8]{3,2,1,0:T(8,128)S(1)} %get-tuple-element.467), channel_id=1, source_target_pairs={{4,0},{8,4},{12,8},{16,12},{20,16},{24,20},{28,24},{32,28},{36,32}... | collective-permute-start | bytes 4616 | tf_op jit(solution)/shard_map/ppermute | solution.py:46
  39.7 2.8 %copy-start = (bf16[6,2,8,2,128,128]{4,5,3,2,1,0:T(8,128)(2,1)S(1)}, bf16[6,2,8,2,128,128]{4,5,3,2,1,0:T(8,128)(2,1)}, u32[]{:S(2)}) copy-start(bf16[6,2,8,2,128,128]{4,5,3,2,1,0:T(8,128)(2,1)} %fusion.68) | copy-start | bytes 18874372
  165.9 8.7 %all-to-all-start.1 = ((f32[4,1,576]{2,1,0:T(1,128)}), f32[4,1,576]{2,1,0:T(1,128)S(1)}, u32[]{:S(2)}, u32[]{:S(2)}) async-start(f32[4,1,576]{2,1,0:T(1,128)} %reshape.452), calls=%async_computation.1 | async-start | bytes 20480 | tf_op jit(solution)/shard_map/all_to_all | solution.py:29
  175.7 10.1 %collective-permute-start.1 = (f32[3,3,3,8,8]{4,3,1,0,2:T(8,128)S(1)}, f32[3,3,3,8,8]{4,3,1,0,2:T(8,128)S(1)}, u32[]{:S(2)}, u32[]{:S(2)}) collective-permute-start(f32[3,3,3,8,8]{4,3,1,0,2:T(8,128)S(1)} %pad_maximum_fusion.2), channel_id=1, source_target_pairs={{0,4},{4,8},{8,12},{12,16},{16,20},{20,24},{24,28},{28,32},{32,36}... | collective-permute-start | bytes 20744 | tf_op jit(solution)/shard_map/ppermute | solution.py:18
  186.1 9.7 %collective-permute-start.4 = (f32[2,3,8,8]{3,2,1,0:T(8,128)S(1)}, f32[2,3,8,8]{3,2,1,0:T(8,128)S(1)}, u32[]{:S(2)}, u32[]{:S(2)}) collective-permute-start(f32[2,3,8,8]{3,2,1,0:T(8,128)S(1)} %get-tuple-element.460), channel_id=1, source_target_pairs={{0,4},{4,8},{8,12},{12,16},{16,20},{20,24},{24,28},{28,32},{32,36}... | collective-permute-start | bytes 4616 | tf_op jit(solution)/shard_map/ppermute | solution.py:43
  193.7 8.5 %collective-permute-start.5 = (f32[2,3,8,8]{3,2,1,0:T(8,128)S(1)}, f32[2,3,8,8]{3,2,1,0:T(8,128)S(1)}, u32[]{:S(2)}, u32[]{:S(2)}) collective-permute-start(f32[2,3,8,8]{3,2,1,0:T(8,128)S(1)} %get-tuple-element.461), channel_id=1, source_target_pairs={{4,0},{8,4},{12,8},{16,12},{20,16},{24,20},{28,24},{32,28},{36,32}... | collective-permute-start | bytes 4616 | tf_op jit(solution)/shard_map/ppermute | solution.py:46
  202.4 4.4 %collective-permute-start.6 = (f32[2,3,8,8]{3,2,1,0:T(8,128)S(1)}, f32[2,3,8,8]{3,2,1,0:T(8,128)S(1)}, u32[]{:S(2)}, u32[]{:S(2)}) collective-permute-start(f32[2,3,8,8]{3,2,1,0:T(8,128)S(1)} %get-tuple-element.454), channel_id=1, source_target_pairs={{0,4},{4,8},{8,12},{12,16},{16,20},{20,24},{24,28},{28,32},{32,36}... | collective-permute-start | bytes 4616 | tf_op jit(solution)/shard_map/ppermute | solution.py:43
  204.3 8.5 %collective-permute-start.7 = (f32[2,3,8,8]{3,2,1,0:T(8,128)S(1)}, f32[2,3,8,8]{3,2,1,0:T(8,128)S(1)}, u32[]{:S(2)}, u32[]{:S(2)}) collective-permute-start(f32[2,3,8,8]{3,2,1,0:T(8,128)S(1)} %get-tuple-element.455), channel_id=1, source_target_pairs={{4,0},{8,4},{12,8},{16,12},{20,16},{24,20},{28,24},{32,28},{36,32}... | collective-permute-start | bytes 4616 | tf_op jit(solution)/shard_map/ppermute | solution.py:46
  213.0 4.4 %collective-permute-start.8 = (f32[2,3,8,8]{3,2,1,0:T(8,128)S(1)}, f32[2,3,8,8]{3,2,1,0:T(8,128)S(1)}, u32[]{:S(2)}, u32[]{:S(2)}) collective-permute-start(f32[2,3,8,8]{3,2,1,0:T(8,128)S(1)} %get-tuple-element.448), channel_id=1, source_target_pairs={{0,4},{4,8},{8,12},{12,16},{16,20},{20,24},{24,28},{28,32},{32,36}... | collective-permute-start | bytes 4616 | tf_op jit(solution)/shard_map/ppermute | solution.py:43
  214.9 8.5 %collective-permute-start.9 = (f32[2,3,8,8]{3,2,1,0:T(8,128)S(1)}, f32[2,3,8,8]{3,2,1,0:T(8,128)S(1)}, u32[]{:S(2)}, u32[]{:S(2)}) collective-permute-start(f32[2,3,8,8]{3,2,1,0:T(8,128)S(1)} %get-tuple-element.449), channel_id=1, source_target_pairs={{4,0},{8,4},{12,8},{16,12},{20,16},{24,20},{28,24},{32,28},{36,32}... | collective-permute-start | bytes 4616 | tf_op jit(solution)/shard_map/ppermute | solution.py:46
  223.6 4.4 %collective-permute-start.10 = (f32[2,3,8,8]{3,2,1,0:T(8,128)S(1)}, f32[2,3,8,8]{3,2,1,0:T(8,128)S(1)}, u32[]{:S(2)}, u32[]{:S(2)}) collective-permute-start(f32[2,3,8,8]{3,2,1,0:T(8,128)S(1)} %get-tuple-element.442), channel_id=1, source_target_pairs={{0,4},{4,8},{8,12},{12,16},{16,20},{20,24},{24,28},{28,32},{32,36}... | collective-permute-start | bytes 4616 | tf_op jit(solution)/shard_map/ppermute | solution.py:43
  225.5 8.5 %collective-permute-start.11 = (f32[2,3,8,8]{3,2,1,0:T(8,128)S(1)}, f32[2,3,8,8]{3,2,1,0:T(8,128)S(1)}, u32[]{:S(2)}, u32[]{:S(2)}) collective-permute-start(f32[2,3,8,8]{3,2,1,0:T(8,128)S(1)} %get-tuple-element.443), channel_id=1, source_target_pairs={{4,0},{8,4},{12,8},{16,12},{20,16},{24,20},{28,24},{32,28},{36,32}... | collective-permute-start | bytes 4616 | tf_op jit(solution)/shard_map/ppermute | solution.py:46
  234.2 4.4 %collective-permute-start.12 = (f32[2,3,8,8]{3,2,1,0:T(8,128)S(1)}, f32[2,3,8,8]{3,2,1,0:T(8,128)S(1)}, u32[]{:S(2)}, u32[]{:S(2)}) collective-permute-start(f32[2,3,8,8]{3,2,1,0:T(8,128)S(1)} %get-tuple-element.436), channel_id=1, source_target_pairs={{0,4},{4,8},{8,12},{12,16},{16,20},{20,24},{24,28},{28,32},{32,36}... | collective-permute-start | bytes 4616 | tf_op jit(solution)/shard_map/ppermute | solution.py:43
  236.1 8.5 %collective-permute-start.13 = (f32[2,3,8,8]{3,2,1,0:T(8,128)S(1)}, f32[2,3,8,8]{3,2,1,0:T(8,128)S(1)}, u32[]{:S(2)}, u32[]{:S(2)}) collective-permute-start(f32[2,3,8,8]{3,2,1,0:T(8,128)S(1)} %get-tuple-element.437), channel_id=1, source_target_pairs={{4,0},{8,4},{12,8},{16,12},{20,16},{24,20},{28,24},{32,28},{36,32}... | collective-permute-start | bytes 4616 | tf_op jit(solution)/shard_map/ppermute | solution.py:46
  244.8 4.4 %collective-permute-start.14 = (f32[2,3,8,8]{3,2,1,0:T(8,128)S(1)}, f32[2,3,8,8]{3,2,1,0:T(8,128)S(1)}, u32[]{:S(2)}, u32[]{:S(2)}) collective-permute-start(f32[2,3,8,8]{3,2,1,0:T(8,128)S(1)} %get-tuple-element.430), channel_id=1, source_target_pairs={{0,4},{4,8},{8,12},{12,16},{16,20},{20,24},{24,28},{28,32},{32,36}... | collective-permute-start | bytes 4616 | tf_op jit(solution)/shard_map/ppermute | solution.py:43
  246.7 8.5 %collective-permute-start.15 = (f32[2,3,8,8]{3,2,1,0:T(8,128)S(1)}, f32[2,3,8,8]{3,2,1,0:T(8,128)S(1)}, u32[]{:S(2)}, u32[]{:S(2)}) collective-permute-start(f32[2,3,8,8]{3,2,1,0:T(8,128)S(1)} %get-tuple-element.431), channel_id=1, source_target_pairs={{4,0},{8,4},{12,8},{16,12},{20,16},{24,20},{28,24},{32,28},{36,32}... | collective-permute-start | bytes 4616 | tf_op jit(solution)/shard_map/ppermute | solution.py:46
  255.4 4.4 %collective-permute-start.16 = (f32[2,3,8,8]{3,2,1,0:T(8,128)S(1)}, f32[2,3,8,8]{3,2,1,0:T(8,128)S(1)}, u32[]{:S(2)}, u32[]{:S(2)}) collective-permute-start(f32[2,3,8,8]{3,2,1,0:T(8,128)S(1)} %get-tuple-element.424), channel_id=1, source_target_pairs={{0,4},{4,8},{8,12},{12,16},{16,20},{20,24},{24,28},{28,32},{32,36}... | collective-permute-start | bytes 4616 | tf_op jit(solution)/shard_map/ppermute | solution.py:43
  257.3 8.5 %collective-permute-start.17 = (f32[2,3,8,8]{3,2,1,0:T(8,128)S(1)}, f32[2,3,8,8]{3,2,1,0:T(8,128)S(1)}, u32[]{:S(2)}, u32[]{:S(2)}) collective-permute-start(f32[2,3,8,8]{3,2,1,0:T(8,128)S(1)} %get-tuple-element.425), channel_id=1, source_target_pairs={{4,0},{8,4},{12,8},{16,12},{20,16},{24,20},{28,24},{32,28},{36,32}... | collective-permute-start | bytes 4616 | tf_op jit(solution)/shard_map/ppermute | solution.py:46
where the time goes:
time: 269 us; the launch traced here: 267 us
  starting transfers between devices  63.7 us (24%)
  local copies, waits for them, and re-layouts  63.3 us (24%)
  other arithmetic  62.8 us (23%)
  waiting for transfers between devices  47.6 us (18%)
  matrix products  27 us (10%)
    dynamic_slice x54, local copies, waits for them, and re-layouts, shards(): lax.map(one_section, (own, extended[step + 1:step + 1 + local], weights[:...  45.9 us
    ppermute x8, waiting for transfers between devices, padded(): lax.ppermute(lax.slice_in_dim(block, 0, width, axis=dim), axis, backward)  42.3 us
    convert_element_type x18, other arithmetic, measure(): right = second_spec.astype(jnp.float32)  31.4 us
    ppermute x8, starting transfers between devices, padded(): lax.ppermute(lax.slice_in_dim(block, block.shape[dim] - width, None, axis...  25.8 us
    ppermute x8, starting transfers between devices, padded(): lax.ppermute(lax.slice_in_dim(block, 0, width, axis=dim), axis, backward)  18.4 us
    dot_general x18, matrix products, measure(): jnp.einsum('arj,...rjk->...ak', tabs[3], back, preferred_element_type=jnp...  18 us
    unnamed x12, local copies, waits for them, and re-layouts  12.3 us
    dynamic_update_slice x18, other arithmetic, shards(): lax.map(one_section, (own, extended[step + 1:step + 1 + local], weights[:...  11.8 us
  transfers between devices with their start and end apart: 20, of which 9 were waited for; matrix products, arithmetic and copies ran while one was open for 55% of the time, Pallas kernels for 0%

commit v1 on v0

v1 whole, which is shorter than its diff:
```python
import functools

import jax
import jax.numpy as jnp
import ml_dtypes
import numpy as np
from jax import lax
from jax.experimental import pallas as pl
from jax.experimental.pallas import tpu as pltpu
from jax.sharding import PartitionSpec as P

SWEEPS = 8
STEP_SIZE = 0.08
EPSILON = 1e-06
LENGTH = 128
HALF = 64
LANES = 128
FULL = 80


def tables():
    index = np.arange(LENGTH)
    phase = (index[:, None] * index[None, :] % LENGTH) * (2.0 * np.pi / LENGTH)
    cosine, sine = np.cos(phase), np.sin(phase)
    shifts = np.where(index < HALF, index, index - LENGTH).astype(np.float64)
    rows = np.zeros((144, LENGTH))
    rows[:HALF] = cosine[:HALF]
    rows[HALF:LENGTH] = sine[:HALF]
    rows[LENGTH] = cosine[HALF]
    cols = np.block([[cosine, -sine], [-sine, -cosine]])
    back = np.block([[cosine, sine], [-sine, cosine]])
    basis = np.concatenate([2.0 * cosine[:, :HALF], -2.0 * sine[:, :HALF]], axis=1)
    basis[:, 0] = 1.0
    basis[:, HALF] = cosine[:, HALF]
    form = basis.T @ (shifts[:, None] * basis)
    cos_part = np.arange(LENGTH) <= HALF
    half_form = np.where(cos_part[None, :], form, 2.0 * form)
    weigh = np.zeros((FULL, LENGTH))
    weigh[: HALF + 1] = half_form[: HALF + 1]
    weigh = np.where(np.abs(weigh) < 1e-6, 0.0, weigh)
    return tuple(t.astype(ml_dtypes.bfloat16) for t in (rows, cols, back, weigh))


def dot(a, b):
    return lax.dot_general(a, b, (((1,), (0,)), ((), ())), preferred_element_type=jnp.float32)


def spectra(patches, rows_ref, cols_ref):
    part = dot(rows_ref[...], jnp.concatenate(patches, axis=1)).astype(jnp.bfloat16)
    stacked = []
    for s in range(len(patches)):
        lanes = slice(s * LANES, (s + 1) * LANES)
        stacked.append(jnp.concatenate([part[:HALF, lanes], part[HALF:LENGTH, lanes]], axis=1))
        stacked.append(
            jnp.concatenate([part[LENGTH:, lanes], jnp.zeros((16, LANES), jnp.bfloat16)], axis=1)
        )
    return dot(jnp.concatenate(stacked, axis=0), cols_ref[...]).astype(jnp.bfloat16)


def cross(a, b):
    a = a[:72].astype(jnp.float32)
    b = b[:72].astype(jnp.float32)
    ar, ai = a[:, :LANES], a[:, LANES:]
    br, bi = b[:, :LANES], b[:, LANES:]
    real = ar * br + ai * bi
    imag = ar * bi - ai * br
    top_real = real[:8] - imag[HALF:]
    top_imag = imag[:8] + real[HALF:]
    real = jnp.concatenate([top_real, real[8:HALF]], axis=0)
    imag = jnp.concatenate([top_imag, imag[8:HALF]], axis=0)
    return jnp.concatenate([real, imag], axis=1).astype(jnp.bfloat16)


def tile_sum(values):
    total = values[0:8]
    for v in range(1, HALF // 8):
        total = total + values[8 * v : 8 * v + 8]
    return total


def moments(pairs, back_ref, weigh_ref, places):
    count = len(pairs)
    back = dot(jnp.concatenate(pairs, axis=0), back_ref[...])
    reals = [back[HALF * n : HALF * n + HALF, :LANES] for n in range(count)]
    imags = [back[HALF * n : HALF * n + HALF, LANES:] for n in range(count)]
    stacked = jnp.concatenate(
        [jnp.concatenate([r, i], axis=0).astype(jnp.bfloat16) for r, i in zip(reals, imags)], axis=1
    )
    weighed = dot(weigh_ref[...], stacked)
    first = lax.broadcasted_iota(jnp.int32, (8, LANES), 0) == 0
    powers = [jnp.zeros((1, LANES), jnp.float32)] * 24
    alongs = list(powers)
    for n in range(count):
        real, imag = reals[n], imags[n]
        square = real * real + imag * imag
        power = 2.0 * tile_sum(square) - jnp.where(first, square[:8], 0.0)
        lanes = slice(n * LANES, (n + 1) * LANES)
        along = tile_sum(real * weighed[:HALF, lanes]) + imag[:8] * weighed[HALF:72, lanes]
        powers[places[n]] = jnp.sum(power, axis=0, keepdims=True)
        alongs[places[n]] = jnp.sum(along, axis=0, keepdims=True)
    power = jnp.concatenate(powers, axis=0)
    along = jnp.concatenate(alongs, axis=0)
    place = lax.broadcasted_iota(jnp.int32, (24, LANES), 1)
    shift = jnp.where(place < HALF, place, place - LENGTH).astype(jnp.float32)
    total = jnp.sum(power, axis=1, keepdims=True) * 2.0**-49 + EPSILON
    by_rows = jnp.sum(along, axis=1, keepdims=True) * 2.0**-56
    by_cols = jnp.sum(power * shift, axis=1, keepdims=True) * 2.0**-49
    return by_rows / total, by_cols / total


def put(acc_ref, node, values):
    lane = lax.broadcasted_iota(jnp.int32, (24, LANES), 1)
    acc_ref[...] = jnp.where(
        lane == node, values[0], jnp.where(lane == node + HALF, values[1], acc_ref[...])
    )


def own_kernel(patches_ref, rows_ref, cols_ref, back_ref, weigh_ref, acc_ref, kept_ref):
    node = pl.program_id(0)

    @pl.when(node == 0)
    def _():
        acc_ref[...] = jnp.zeros_like(acc_ref)

    spec = spectra([patches_ref[s, 0] for s in range(6)], rows_ref, cols_ref)
    specs = [spec[FULL * s : FULL * s + FULL] for s in range(6)]
    for s in range(3):
        kept_ref[0, s] = specs[3 + s]
    chosen = [(s, o) for o in (1, 2, 3) for s in range(6 - o)]
    pairs = [cross(specs[s], specs[s + o]) for s, o in chosen]
    put(acc_ref, node, moments(pairs, back_ref, weigh_ref, [8 * (o - 1) + s for s, o in chosen]))


def next_kernel(
    tile_ref, patches_ref, kept_ref, rows_ref, cols_ref, back_ref, weigh_ref,
    own_ref, weights_ref, nodes_ref, measured_ref, message_ref,
):
    node = pl.program_id(0)

    @pl.when(node == 0)
    def _():
        measured_ref[...] = own_ref[...]

    spec = spectra([patches_ref[s, 0] for s in range(3)], rows_ref, cols_ref)
    ahead = [spec[FULL * s : FULL * s + FULL] for s in range(3)]
    chosen = [(s, o) for o in (1, 2, 3) for s in range(6 - o, 6)]
    pairs = [cross(kept_ref[0, s - 3], ahead[s + o - 6]) for s, o in chosen]
    place = [8 * (o - 1) + s for s, o in chosen]
    row = lax.broadcasted_iota(jnp.int32, (24, LANES), 0)
    mine = functools.reduce(jnp.logical_or, [row == p for p in place])
    lane = lax.broadcasted_iota(jnp.int32, (24, LANES), 1)
    by_rows, by_cols = moments(pairs, back_ref, weigh_ref, place)
    old = measured_ref[...]
    new = jnp.where(mine & (lane == node), by_rows, old)
    measured_ref[...] = jnp.where(mine & (lane == node + HALF), by_cols, new)

    @pl.when(node == pl.num_programs(0) - 1)
    def _():
        measured = measured_ref[...] * weights_ref[...]
        measured_ref[...] = measured
        turn = tile_ref[0] * 16
        row = lax.broadcasted_iota(jnp.int32, (8, LANES), 0)
        zero = jnp.zeros((8, LANES), jnp.float32)
        low = jnp.zeros((16, LANES), jnp.float32)
        for o in (1, 2, 3):
            part = measured[8 * o - 8 : 8 * o]
            wide = jnp.concatenate([part, zero], axis=0)
            low = low - wide + pltpu.roll(wide, o, 0)
        lane = lax.broadcasted_iota(jnp.int32, (8, LANES), 1)
        flags = zero
        for o in (1, 2, 3):
            flags = jnp.where(lane == o - 1, weights_ref[8 * o - 8 : 8 * o], flags)
        message = jnp.concatenate([nodes_ref[...], flags, low], axis=0)
        message_ref[...] = pltpu.roll(message, turn, 1)


def relax_kernel(tile_ref, near_ref, low_ref, high_ref, out_ref, u_ref, w_ref, b_ref):
    u_ref[...] = jnp.zeros_like(u_ref)
    w_ref[...] = jnp.zeros_like(w_ref)
    b_ref[...] = jnp.zeros_like(b_ref)
    for trio, centre in ((low_ref, 1), (near_ref, 4), (high_ref, 7)):
        for part, by in ((0, 0), (1, -1), (2, 1)):
            row = 6 * (centre + by)
            u_ref[row : row + 6] = trio[part, 0:6]
            w_ref[row : row + 6] = trio[part, 8:14]
            b_ref[row : row + 9] += trio[part, 16:25]
    u = u_ref[...]
    flags = w_ref[...]
    lane = lax.broadcasted_iota(jnp.int32, u.shape, 1)
    weights = [
        jnp.sum(jnp.where(lane % 16 == o, flags, 0.0)[:, :HALF], axis=1, keepdims=True) * 0.25
        for o in range(3)
    ]
    weights = [jnp.broadcast_to(w, u.shape) for w in weights]
    pull = b_ref[...]
    col = lane % 8
    row = (lane // 8) % 8
    masks = [
        (m.astype(jnp.float32), by)
        for m, by in ((col > 0, 1), (col < 7, LANES - 1), (row > 0, 8), (row < 7, LANES - 8))
    ]
    degree = masks[0][0] + masks[1][0] + masks[2][0] + masks[3][0]
    for _ in range(SWEEPS):
        force = pull - degree * u
        for mask, by in masks:
            force = force + mask * pltpu.roll(u, by, 1)
        for o in (1, 2, 3):
            resid = weights[o - 1] * (pltpu.roll(u, u.shape[0] - o, 0) - u)
            force = force + resid - pltpu.roll(resid, o, 0)
        u = u + STEP_SIZE * force
    u_ref[...] = u
    turn = lax.rem(LANES - tile_ref[0] * 16, LANES)
    out_ref[...] = pltpu.roll(u_ref[24:32], turn, 1)


def shifted(value, axis, by):
    count = lax.axis_size(axis)
    pairs = [(i, i + by) for i in range(count) if 0 <= i + by < count]
    return lax.ppermute(value, axis, pairs)


def turned_by(value, axis, by):
    count = lax.axis_size(axis)
    return lax.ppermute(value, axis, [(i, (i + by) % count) for i in range(count)])


def shards(patches, pair_flags, nodes):
    local, rows_local, columns = patches.shape[:3]
    reach = pair_flags.shape[1]
    count = rows_local * columns
    flat = patches.reshape(local, count, LENGTH, LENGTH)
    tabs = tables()
    received = shifted(flat[:reach], "sec", -1)
    table_specs = [pl.BlockSpec(t.shape, lambda n: (0, 0)) for t in tabs]
    whole = pl.BlockSpec((24, LANES), lambda n: (0, 0))
    params = pltpu.CompilerParams(vmem_limit_bytes=48 * 1024 * 1024)
    own, kept = pl.pallas_call(
        own_kernel,
        grid=(count,),
        in_specs=[pl.BlockSpec((local, 1, LENGTH, LENGTH), lambda n: (0, n, 0, 0)), *table_specs],
        out_specs=[whole, pl.BlockSpec((1, 3, FULL, 2 * LANES), lambda n: (n, 0, 0, 0))],
        out_shape=[
            jax.ShapeDtypeStruct((24, LANES), jnp.float32),
            jax.ShapeDtypeStruct((count, 3, FULL, 2 * LANES), jnp.bfloat16),
        ],
        compiler_params=params,
        cost_estimate=pl.CostEstimate(flops=8_000_000_000, bytes_accessed=6_000_000, transcendentals=0),
        name="own_pairs",
    )(flat, *tabs)

    sections = lax.axis_size("sec") * local
    placed = lax.axis_index("sec") * local + jnp.arange(local, dtype=jnp.int32)
    offsets = jnp.arange(1, reach + 1, dtype=jnp.int32)
    weights = pair_flags.astype(jnp.float32) * (
        placed[:, None] + offsets[None, :] < sections
    ).astype(jnp.float32)
    weight_rows = jnp.broadcast_to(
        jnp.pad(weights.T, ((0, 0), (0, 2)))[:, :, None], (reach, 8, LANES)
    ).reshape(24, LANES)
    node_rows = jnp.pad(
        jnp.transpose(nodes, (1, 0, 2, 3)).reshape(local, 2, count), ((0, 2), (0, 0), (0, HALF - count))
    ).reshape(8, LANES)
    tile = lax.axis_index("tile").astype(jnp.int32).reshape(1)

    smem = pl.BlockSpec(memory_space=pltpu.SMEM)
    measured_rows, message = pl.pallas_call(
        next_kernel,
        grid=(count,),
        in_specs=[
            smem,
            pl.BlockSpec((reach, 1, LENGTH, LENGTH), lambda n: (0, n, 0, 0)),
            pl.BlockSpec((1, 3, FULL, 2 * LANES), lambda n: (n, 0, 0, 0)),
            *table_specs,
            whole,
            whole,
            pl.BlockSpec((8, LANES), lambda n: (0, 0)),
        ],
        out_specs=[whole, pl.BlockSpec((32, LANES), lambda n: (0, 0))],
        out_shape=[
            jax.ShapeDtypeStruct((24, LANES), jnp.float32),
            jax.ShapeDtypeStruct((32, LANES), jnp.float32),
        ],
        compiler_params=params,
        cost_estimate=pl.CostEstimate(flops=4_000_000_000, bytes_accessed=4_000_000, transcendentals=0),
        name="next_pairs",
    )(tile, received, kept, *tabs, own, weight_rows, node_rows)

    joined = message
    for by in range(1, lax.axis_size("tile")):
        joined = joined + turned_by(message, "tile", by)
    near = jnp.stack([joined, turned_by(joined, "sec", 1), turned_by(joined, "sec", -1)], axis=0)
    low = turned_by(near, "sec", 3)
    high = turned_by(near, "sec", -3)
    relaxed_rows = pl.pallas_call(
        relax_kernel,
        in_specs=[smem] + [pl.BlockSpec(memory_space=pltpu.VMEM)] * 3,
        out_specs=pl.BlockSpec(memory_space=pltpu.VMEM),
        out_shape=jax.ShapeDtypeStruct((8, LANES), jnp.float32),
        scratch_shapes=[pltpu.VMEM((64, LANES), jnp.float32)] * 3,
        name="relax",
    )(tile, near, low, high)

    measured = jnp.transpose(
        measured_rows.reshape(reach, 8, 2, HALF)[:, :local, :, :count], (2, 1, 0, 3)
    ).reshape(2, local, reach, rows_local, columns)
    relaxed = jnp.transpose(
        relaxed_rows.reshape(8, 2, HALF)[:local, :, :count], (1, 0, 2)
    ).reshape(2, local, rows_local, columns)
    return relaxed, measured


def solution(mesh):
    placed = (P("sec", "tile", None, None, None), P("sec", None), P(None, "sec", "tile", None))
    return jax.shard_map(
        shards,
        mesh=mesh,
        in_specs=placed,
        out_specs=(P(None, "sec", "tile", None), P(None, "sec", None, "tile", None)),
        check_vma=False,
    )
```

time: 269 us -> 73.1 us (0.27)
  the two profiles are of different devices: /device:TPU:121 before, /device:TPU:8 now
where the time goes in v1:
time: 73.1 us; the launch traced here: 72.4 us
  Pallas kernels  31.3 us (43%)
  starting transfers between devices  17.6 us (24%)
  waiting for transfers between devices  13.3 us (18%)
  local copies, waits for them, and re-layouts  8.68 us (12%)
  other arithmetic  0.77 us (1%)
    ppermute x7, starting transfers between devices, turned_by(): lax.ppermute(value, axis, [(i, (i + by) % count) for i in range(count)])  15.7 us
    pallas_call x1, Pallas kernels, shards(): pl.pallas_call(own_kernel, grid=(count,), in_specs=[pl.BlockSpec((local,...  14.9 us
    pallas_call x1, Pallas kernels, shards(): pl.pallas_call(next_kernel, grid=(count,), in_specs=[smem, pl.BlockSpec((...  14.1 us
    ppermute x7, waiting for transfers between devices, turned_by(): lax.ppermute(value, axis, [(i, (i + by) % count) for i in range(count)])  13.3 us
    unnamed x22, local copies, waits for them, and re-layouts  3.68 us
    slice x1, local copies, waits for them, and re-layouts, shards(): received = shifted(flat[:reach], 'sec', -1)  2.91 us
    pallas_call x1, Pallas kernels, shards(): pl.pallas_call(relax_kernel, in_specs=[smem] + [pl.BlockSpec(memory_space...  2.36 us
    ppermute x1, starting transfers between devices, shifted(): return lax.ppermute(value, axis, pairs)  1.91 us
  transfers between devices with their start and end apart: 8, of which 6 were waited for; matrix products, arithmetic and copies ran while one was open for 4% of the time, Pallas kernels for 21%

profile of v1, /device:TPU:8, one launch (start us, length us, event | category | flops | bytes accessed | tf_op | source)
XLA Modules:
  0.0 72.4 jit_solution(2808237738174924131)
XLA Ops:
  0.6 0.0 copy-start.6
  0.6 0.0 copy-start.5
  0.7 0.0 copy-start
  0.7 2.9 %slice.12 = bf16[3,2,8,128,128]{4,3,2,1,0:T(8,128)(2,1)} slice(bf16[6,2,8,128,128]{4,3,2,1,0:T(8,128)(2,1)} %param.7), slice={[0:3], [0:2], [0:8], [0:128], [0:128]} | slice | bytes 3145728 | tf_op jit(solution)/shard_map/slice | solution.py:233
  3.6 1.9 %collective-permute-start = (bf16[3,16,128,128]{3,2,1,0:T(8,128)(2,1)}, bf16[3,16,128,128]{3,2,1,0:T(8,128)(2,1)}, u32[]{:S(2)}, u32[]{:S(2)}) collective-permute-start(bf16[3,16,128,128]{3,2,1,0:T(8,128)(2,1)} %bitcast.1), channel_id=1, source_target_pairs={{4,0},{8,4},{12,8},{16,12},{20,16},{24,20},{28,24},{32,28},{36,32}... | collective-permute-start | bytes 4718600 | tf_op jit(solution)/shard_map/ppermute | solution.py:219
  5.5 0.8 %select_bitcast_fusion = f32[3,6]{1,0:T(4,128)S(1)} fusion(s32[6,3]{0,1:T(4,128)} %param.8, s32[3]{0:T(128)S(1)} %iota_add_fusion, s32[6]{0:T(128)S(1)} %iota_add_fusion.1), kind=kLoop, calls=%fused_computation.4 | loop fusion | flops 72 | bytes 180 | tf_op jit(solution)/shard_map/transpose | solution.py:258
  6.3 0.1 broadcast_in_dim.4
  6.4 0.8 %reshape.49 = f32[6,2,16]{2,0,1:T(8,128)S(1)} reshape(f32[6,2,2,8]{3,2,0,1:T(2,128)} %bitcast.23) | data formatting | bytes 1536 | tf_op jit(solution)/shard_map/reshape | solution.py:261
  7.2 0.1 reshape.44.nodes_ref
  7.3 0.0 copy-done.6
  7.3 0.0 copy-done.5
  7.3 0.0 copy-done
  7.3 0.0 copy-start.1
  7.3 0.9 %copy-done.1 = bf16[256,256]{1,0:T(8,128)(2,1)S(1)} copy-done((bf16[256,256]{1,0:T(8,128)(2,1)S(1)}, bf16[256,256]{1,0:T(8,128)(2,1)}, u32[]{:S(2)}) %copy-start.1) | copy-done | bytes 131096
  8.2 0.0 copy-start.3
  8.2 0.9 %copy-done.3 = bf16[256,256]{1,0:T(8,128)(2,1)S(1)} copy-done((bf16[256,256]{1,0:T(8,128)(2,1)S(1)}, bf16[256,256]{1,0:T(8,128)(2,1)}, u32[]{:S(2)}) %copy-start.3) | copy-done | bytes 131096
  9.1 0.0 copy-start.2
  9.1 0.0 copy-start.4
  9.1 14.9 %own_pairs.1 = (f32[24,128]{1,0:T(8,128)S(1)}, bf16[16,3,80,256]{3,2,1,0:T(8,128)(2,1)S(1)}) custom-call(bf16[6,16,128,128]{3,2,1,0:T(8,128)(2,1)S(1)} %bitcast.19, bf16[144,128]{1,0:T(8,128)(2,1)S(1)} %copy-done.5, bf16[256,256]{1,0:T(8,128)(2,1)S(1)} %copy-done.3, bf16[256,256]{1,0:T(8,128)(2,1)S(1)} %copy-done.1, bf16[80,128]{1,0:T(8,128)(2,1)S(1)} %copy-done.6), custom_call_target="tpu_custom_call" | custom-call | flops 8000000000 | bytes 6000000 | tf_op jit(solution)/shard_map/own_pairs/pallas_call | solution.py:237
  23.9 0.0 collective-permute-done.patches_ref
  23.9 0.1 broadcast_in_dim.5.weights_ref
  24.0 0.0 copy-done.2
  24.0 0.0 copy-done.4
  24.0 14.1 %next_pairs.1 = (f32[24,128]{1,0:T(8,128)S(1)}, f32[32,128]{1,0:T(8,128)S(1)}) custom-call(s32[1]{0:T(128)} %bitcast.tile_ref, bf16[3,16,128,128]{3,2,1,0:T(8,128)(2,1)} %collective-permute-done.patches_ref, bf16[16,3,80,256]{3,2,1,0:T(8,128)(2,1)S(1)} %get-tuple-element.6.kept_ref, bf16[144,128]{1,0:T(8,128)(2,1)S(1)} %copy-done.5, ...), custom_call_target="tpu_custom_call" | custom-call | flops 4000000000 | bytes 4000000 | tf_op jit(solution)/shard_map/next_pairs/pallas_call | solution.py:266
  38.1 2.8 %collective-permute-start.3 = (f32[32,128]{1,0:T(8,128)S(1)}, f32[32,128]{1,0:T(8,128)S(1)}, u32[]{:S(2)}, u32[]{:S(2)}) collective-permute-start(f32[32,128]{1,0:T(8,128)S(1)} %get-tuple-element.8), channel_id=1, source_target_pairs={{0,3},{1,0},{2,1},{3,2},{4,7},{5,4},{6,5},{7,6},{8,11},{9,8},{10,9... | collective-permute-start | bytes 49160 | tf_op jit(solution)/shard_map/ppermute | solution.py:224
  40.9 0.8 %collective-permute-start.2 = (f32[32,128]{1,0:T(8,128)S(1)}, f32[32,128]{1,0:T(8,128)S(1)}, u32[]{:S(2)}, u32[]{:S(2)}) collective-permute-start(f32[32,128]{1,0:T(8,128)S(1)} %get-tuple-element.8), channel_id=1, source_target_pairs={{0,2},{1,3},{2,0},{3,1},{4,6},{5,7},{6,4},{7,5},{8,10},{9,11},{10,... | collective-permute-start | bytes 49160 | tf_op jit(solution)/shard_map/ppermute | solution.py:224
  41.7 0.9 %collective-permute-start.1 = (f32[32,128]{1,0:T(8,128)S(1)}, f32[32,128]{1,0:T(8,128)S(1)}, u32[]{:S(2)}, u32[]{:S(2)}) collective-permute-start(f32[32,128]{1,0:T(8,128)S(1)} %get-tuple-element.8), channel_id=1, source_target_pairs={{0,1},{1,2},{2,3},{3,0},{4,5},{5,6},{6,7},{7,4},{8,9},{9,10},{10,1... | collective-permute-start | bytes 49160 | tf_op jit(solution)/shard_map/ppermute | solution.py:224
  42.6 0.0 collective-permute-done.3
  42.6 3.6 %collective-permute-done.2 = f32[32,128]{1,0:T(8,128)S(1)} collective-permute-done((f32[32,128]{1,0:T(8,128)S(1)}, f32[32,128]{1,0:T(8,128)S(1)}, u32[]{:S(2)}, u32[]{:S(2)}) %collective-permute-start.2) | collective-permute-done | bytes 16416 | tf_op jit(solution)/shard_map/ppermute | solution.py:224
  46.2 0.7 collective-permute-done.1
  46.9 0.0 collective-permute-start.5
  46.9 0.5 collective-permute-start.4
  47.4 0.1 reshape.47
  47.4 0.9 %collective-permute-done.5 = f32[32,128]{1,0:T(8,128)S(1)} collective-permute-done((f32[32,128]{1,0:T(8,128)S(1)}, f32[32,128]{1,0:T(8,128)S(1)}, u32[]{:S(2)}, u32[]{:S(2)}) %collective-permute-start.5) | collective-permute-done | bytes 16416 | tf_op jit(solution)/shard_map/ppermute | solution.py:224
  48.3 1.8 %collective-permute-done.4 = f32[32,128]{1,0:T(8,128)S(1)} collective-permute-done((f32[32,128]{1,0:T(8,128)S(1)}, f32[32,128]{1,0:T(8,128)S(1)}, u32[]{:S(2)}, u32[]{:S(2)}) %collective-permute-start.4) | collective-permute-done | bytes 16416 | tf_op jit(solution)/shard_map/ppermute | solution.py:224
  50.1 0.0 copy-start.7
  50.1 10.7 %collective-permute-start.7 = (f32[3,32,128]{2,1,0:T(8,128)S(1)}, f32[3,32,128]{2,1,0:T(8,128)S(1)}, u32[]{:S(2)}, u32[]{:S(2)}) collective-permute-start(f32[3,32,128]{2,1,0:T(8,128)S(1)} %pad_maximum_fusion.near_ref), channel_id=1, source_target_pairs={{0,244},{4,248},{8,252},{12,0},{16,4},{20,8},{24,12},{28,16},{32,2... | collective-permute-start | bytes 147464 | tf_op jit(solution)/shard_map/ppermute | solution.py:224
  60.8 0.0 collective-permute-start.6
  60.8 0.1 reshape.48
  60.9 0.6 copy.15
  61.6 1.0 %collective-permute-done.7.high_ref = f32[3,32,128]{2,1,0:T(8,128)S(1)} collective-permute-done((f32[3,32,128]{2,1,0:T(8,128)S(1)}, f32[3,32,128]{2,1,0:T(8,128)S(1)}, u32[]{:S(2)}, u32[]{:S(2)}) %collective-permute-start.7) | collective-permute-done | bytes 49184 | tf_op jit(solution)/shard_map/ppermute | solution.py:224
  62.6 0.0 copy-start.8
  62.6 5.4 %collective-permute-done.6.low_ref = f32[3,32,128]{2,1,0:T(8,128)S(1)} collective-permute-done((f32[3,32,128]{2,1,0:T(8,128)S(1)}, f32[3,32,128]{2,1,0:T(8,128)S(1)}, u32[]{:S(2)}, u32[]{:S(2)}) %collective-permute-start.6) | collective-permute-done | bytes 49184 | tf_op jit(solution)/shard_map/ppermute | solution.py:224
  68.0 0.0 copy-done.7
  68.0 0.0 copy-done.8
  68.0 0.0 copy-start.9
  68.0 0.6 copy-done.9
  68.6 2.4 %relax.1 = f32[8,128]{1,0:T(8,128)} custom-call(s32[1]{0:T(128)} %bitcast.tile_ref, f32[3,32,128]{2,1,0:T(8,128)} %copy-done.7, f32[3,32,128]{2,1,0:T(8,128)} %copy-done.9, f32[3,32,128]{2,1,0:T(8,128)} %copy-done.8), custom_call_target="tpu_custom_call" | custom-call | tf_op jit(solution)/shard_map/relax/pallas_call | solution.py:294
  70.9 0.8 %reshape.45 = f32[8,2,64]{2,1,0:T(2,128)S(1)} reshape(f32[8,128]{1,0:T(8,128)} %relax.1) | data formatting | bytes 8192 | tf_op jit(solution)/shard_map/reshape | solution.py:307
  71.7 0.1 reshape.46
  71.8 0.6 copy.14
  (9 shorter events, 0.1 us)
Async XLA Ops:
  0.6 6.6 %copy-start.6 = (bf16[80,128]{1,0:T(8,128)(2,1)S(1)}, bf16[80,128]{1,0:T(8,128)(2,1)}, u32[]{:S(2)}) copy-start(bf16[80,128]{1,0:T(8,128)(2,1)} %constant.30.clone.weigh_ref) | copy-start | bytes 61444
  0.6 6.6 %copy-start.5 = (bf16[144,128]{1,0:T(8,128)(2,1)S(1)}, bf16[144,128]{1,0:T(8,128)(2,1)}, u32[]{:S(2)}) copy-start(bf16[144,128]{1,0:T(8,128)(2,1)} %constant.27.clone.rows_ref) | copy-start | bytes 110596
  0.7 6.6 %copy-start = (bf16[6,2,8,128,128]{4,3,2,1,0:T(8,128)(2,1)S(1)}, bf16[6,2,8,128,128]{4,3,2,1,0:T(8,128)(2,1)}, u32[]{:S(2)}) copy-start(bf16[6,2,8,128,128]{4,3,2,1,0:T(8,128)(2,1)} %param.7) | copy-start | bytes 9437188
  3.6 20.4 %collective-permute-start = (bf16[3,16,128,128]{3,2,1,0:T(8,128)(2,1)}, bf16[3,16,128,128]{3,2,1,0:T(8,128)(2,1)}, u32[]{:S(2)}, u32[]{:S(2)}) collective-permute-start(bf16[3,16,128,128]{3,2,1,0:T(8,128)(2,1)} %bitcast.1), channel_id=1, source_target_pairs={{4,0},{8,4},{12,8},{16,12},{20,16},{24,20},{28,24},{32,28},{36,32}... | collective-permute-start | bytes 4718600 | tf_op jit(solution)/shard_map/ppermute | solution.py:219
  7.3 0.9 %copy-start.1 = (bf16[256,256]{1,0:T(8,128)(2,1)S(1)}, bf16[256,256]{1,0:T(8,128)(2,1)}, u32[]{:S(2)}) copy-start(bf16[256,256]{1,0:T(8,128)(2,1)} %constant.29.clone.back_ref) | copy-start | bytes 393220
  8.2 0.9 %copy-start.3 = (bf16[256,256]{1,0:T(8,128)(2,1)S(1)}, bf16[256,256]{1,0:T(8,128)(2,1)}, u32[]{:S(2)}) copy-start(bf16[256,256]{1,0:T(8,128)(2,1)} %constant.28.clone.cols_ref) | copy-start | bytes 393220
  9.1 14.9 %copy-start.2 = (bf16[256,256]{1,0:T(8,128)(2,1)S(1)}, bf16[256,256]{1,0:T(8,128)(2,1)}, u32[]{:S(2)}) copy-start(bf16[256,256]{1,0:T(8,128)(2,1)} %constant.29.clone.back_ref) | copy-start | bytes 393220
  9.1 14.9 %copy-start.4 = (bf16[256,256]{1,0:T(8,128)(2,1)S(1)}, bf16[256,256]{1,0:T(8,128)(2,1)}, u32[]{:S(2)}) copy-start(bf16[256,256]{1,0:T(8,128)(2,1)} %constant.28.clone.cols_ref) | copy-start | bytes 393220
  38.1 4.5 %collective-permute-start.3 = (f32[32,128]{1,0:T(8,128)S(1)}, f32[32,128]{1,0:T(8,128)S(1)}, u32[]{:S(2)}, u32[]{:S(2)}) collective-permute-start(f32[32,128]{1,0:T(8,128)S(1)} %get-tuple-element.8), channel_id=1, source_target_pairs={{0,3},{1,0},{2,1},{3,2},{4,7},{5,4},{6,5},{7,6},{8,11},{9,8},{10,9... | collective-permute-start | bytes 49160 | tf_op jit(solution)/shard_map/ppermute | solution.py:224
  40.9 5.2 %collective-permute-start.2 = (f32[32,128]{1,0:T(8,128)S(1)}, f32[32,128]{1,0:T(8,128)S(1)}, u32[]{:S(2)}, u32[]{:S(2)}) collective-permute-start(f32[32,128]{1,0:T(8,128)S(1)} %get-tuple-element.8), channel_id=1, source_target_pairs={{0,2},{1,3},{2,0},{3,1},{4,6},{5,7},{6,4},{7,5},{8,10},{9,11},{10,... | collective-permute-start | bytes 49160 | tf_op jit(solution)/shard_map/ppermute | solution.py:224
  41.7 5.1 %collective-permute-start.1 = (f32[32,128]{1,0:T(8,128)S(1)}, f32[32,128]{1,0:T(8,128)S(1)}, u32[]{:S(2)}, u32[]{:S(2)}) collective-permute-start(f32[32,128]{1,0:T(8,128)S(1)} %get-tuple-element.8), channel_id=1, source_target_pairs={{0,1},{1,2},{2,3},{3,0},{4,5},{5,6},{6,7},{7,4},{8,9},{9,10},{10,1... | collective-permute-start | bytes 49160 | tf_op jit(solution)/shard_map/ppermute | solution.py:224
  46.9 1.4 %collective-permute-start.5 = (f32[32,128]{1,0:T(8,128)S(1)}, f32[32,128]{1,0:T(8,128)S(1)}, u32[]{:S(2)}, u32[]{:S(2)}) collective-permute-start(f32[32,128]{1,0:T(8,128)S(1)} %add_add_fusion), channel_id=1, source_target_pairs={{0,252},{4,0},{8,4},{12,8},{16,12},{20,16},{24,20},{28,24},{32,28}... | collective-permute-start | bytes 49160 | tf_op jit(solution)/shard_map/ppermute | solution.py:224
  46.9 3.2 %collective-permute-start.4 = (f32[32,128]{1,0:T(8,128)S(1)}, f32[32,128]{1,0:T(8,128)S(1)}, u32[]{:S(2)}, u32[]{:S(2)}) collective-permute-start(f32[32,128]{1,0:T(8,128)S(1)} %add_add_fusion), channel_id=1, source_target_pairs={{0,4},{4,8},{8,12},{12,16},{16,20},{20,24},{24,28},{28,32},{32,36}... | collective-permute-start | bytes 49160 | tf_op jit(solution)/shard_map/ppermute | solution.py:224
  50.1 17.9 %copy-start.7 = (f32[3,32,128]{2,1,0:T(8,128)}, f32[3,32,128]{2,1,0:T(8,128)S(1)}, u32[]{:S(2)}) copy-start(f32[3,32,128]{2,1,0:T(8,128)S(1)} %pad_maximum_fusion.near_ref) | copy-start | bytes 147460
  50.1 12.5 %collective-permute-start.7 = (f32[3,32,128]{2,1,0:T(8,128)S(1)}, f32[3,32,128]{2,1,0:T(8,128)S(1)}, u32[]{:S(2)}, u32[]{:S(2)}) collective-permute-start(f32[3,32,128]{2,1,0:T(8,128)S(1)} %pad_maximum_fusion.near_ref), channel_id=1, source_target_pairs={{0,244},{4,248},{8,252},{12,0},{16,4},{20,8},{24,12},{28,16},{32,2... | collective-permute-start | bytes 147464 | tf_op jit(solution)/shard_map/ppermute | solution.py:224
  60.8 7.1 %collective-permute-start.6 = (f32[3,32,128]{2,1,0:T(8,128)S(1)}, f32[3,32,128]{2,1,0:T(8,128)S(1)}, u32[]{:S(2)}, u32[]{:S(2)}) collective-permute-start(f32[3,32,128]{2,1,0:T(8,128)S(1)} %pad_maximum_fusion.near_ref), channel_id=1, source_target_pairs={{0,12},{4,16},{8,20},{12,24},{16,28},{20,32},{24,36},{28,40},{32,4... | collective-permute-start | bytes 147464 | tf_op jit(solution)/shard_map/ppermute | solution.py:224
  62.6 5.4 %copy-start.8 = (f32[3,32,128]{2,1,0:T(8,128)}, f32[3,32,128]{2,1,0:T(8,128)S(1)}, u32[]{:S(2)}) copy-start(f32[3,32,128]{2,1,0:T(8,128)S(1)} %collective-permute-done.7.high_ref) | copy-start | bytes 147460
  68.0 0.6 copy-start.9

commit v2 on v1

--- a/solution.py
+++ b/solution.py
@@ -15,6 +15,8 @@
 LENGTH = 128
 HALF = 64
 LANES = 128
+OWN_NODES = 8
+NEXT_NODES = 8
 FULL = 80
 
 
@@ -78,7 +80,7 @@
     return total
 
 
-def moments(pairs, back_ref, weigh_ref, places):
+def moments(pairs, back_ref, weigh_ref):
     count = len(pairs)
     back = dot(jnp.concatenate(pairs, axis=0), back_ref[...])
     reals = [back[HALF * n : HALF * n + HALF, :LANES] for n in range(count)]
@@ -88,18 +90,23 @@
     )
     weighed = dot(weigh_ref[...], stacked)
     first = lax.broadcasted_iota(jnp.int32, (8, LANES), 0) == 0
-    powers = [jnp.zeros((1, LANES), jnp.float32)] * 24
-    alongs = list(powers)
+    powers, alongs = [], []
     for n in range(count):
         real, imag = reals[n], imags[n]
         square = real * real + imag * imag
         power = 2.0 * tile_sum(square) - jnp.where(first, square[:8], 0.0)
         lanes = slice(n * LANES, (n + 1) * LANES)
         along = tile_sum(real * weighed[:HALF, lanes]) + imag[:8] * weighed[HALF:72, lanes]
-        powers[places[n]] = jnp.sum(power, axis=0, keepdims=True)
-        alongs[places[n]] = jnp.sum(along, axis=0, keepdims=True)
-    power = jnp.concatenate(powers, axis=0)
-    along = jnp.concatenate(alongs, axis=0)
+        powers.append(jnp.sum(power, axis=0, keepdims=True))
+        alongs.append(jnp.sum(along, axis=0, keepdims=True))
+    return powers, alongs
+
+
+def shifts_of(powers, alongs, places):
+    zero = jnp.zeros((1, LANES), jnp.float32)
+    at = dict(zip(places, range(len(places))))
+    power = jnp.concatenate([powers[at[r]] if r in at else zero for r in range(24)], axis=0)
+    along = jnp.concatenate([alongs[at[r]] if r in at else zero for r in range(24)], axis=0)
     place = lax.broadcasted_iota(jnp.int32, (24, LANES), 1)
     shift = jnp.where(place < HALF, place, place - LENGTH).astype(jnp.float32)
     total = jnp.sum(power, axis=1, keepdims=True) * 2.0**-49 + EPSILON
@@ -108,53 +115,66 @@
     return by_rows / total, by_cols / total
 
 
-def put(acc_ref, node, values):
+def put_shifts(acc, step, nodes, pairs, back_ref, weigh_ref, places):
+    powers, alongs = moments(pairs, back_ref, weigh_ref)
     lane = lax.broadcasted_iota(jnp.int32, (24, LANES), 1)
-    acc_ref[...] = jnp.where(
-        lane == node, values[0], jnp.where(lane == node + HALF, values[1], acc_ref[...])
-    )
+    each = len(places)
+    for k in range(nodes):
+        mine = slice(k * each, (k + 1) * each)
+        by_rows, by_cols = shifts_of(powers[mine], alongs[mine], places)
+        node = step * nodes + k
+        here = jnp.where(lane == node, by_rows, jnp.where(lane == node + HALF, by_cols, 0.0))
+        acc = acc + here
+    return acc
 
 
 def own_kernel(patches_ref, rows_ref, cols_ref, back_ref, weigh_ref, acc_ref, kept_ref):
-    node = pl.program_id(0)
-
-    @pl.when(node == 0)
+    step = pl.program_id(0)
+    nodes = patches_ref.shape[1]
+
+    @pl.when(step == 0)
     def _():
         acc_ref[...] = jnp.zeros_like(acc_ref)
 
-    spec = spectra([patches_ref[s, 0] for s in range(6)], rows_ref, cols_ref)
-    specs = [spec[FULL * s : FULL * s + FULL] for s in range(6)]
-    for s in range(3):
-        kept_ref[0, s] = specs[3 + s]
+    spec = spectra(
+        [patches_ref[s, k] for k in range(nodes) for s in range(6)], rows_ref, cols_ref
+    )
     chosen = [(s, o) for o in (1, 2, 3) for s in range(6 - o)]
-    pairs = [cross(specs[s], specs[s + o]) for s, o in chosen]
-    put(acc_ref, node, moments(pairs, back_ref, weigh_ref, [8 * (o - 1) + s for s, o in chosen]))
+    pairs = []
+    for k in range(nodes):
+        specs = [spec[FULL * (6 * k + s) : FULL * (6 * k + s) + FULL] for s in range(6)]
+        for s in range(3):
+            kept_ref[k, s] = specs[3 + s]
+        pairs += [cross(specs[s], specs[s + o]) for s, o in chosen]
+    acc_ref[...] = put_shifts(
+        acc_ref[...], step, nodes, pairs, back_ref, weigh_ref, [8 * (o - 1) + s for s, o in chosen]
+    )
 
 
 def next_kernel(
     tile_ref, patches_ref, kept_ref, rows_ref, cols_ref, back_ref, weigh_ref,
     own_ref, weights_ref, nodes_ref, measured_ref, message_ref,
 ):
-    node = pl.program_id(0)
-
-    @pl.when(node == 0)
+    step = pl.program_id(0)
+    nodes = patches_ref.shape[1]
+
+    @pl.when(step == 0)
     def _():
         measured_ref[...] = own_ref[...]
 
-    spec = spectra([patches_ref[s, 0] for s in range(3)], rows_ref, cols_ref)
-    ahead = [spec[FULL * s : FULL * s + FULL] for s in range(3)]
+    spec = spectra(
+        [patches_ref[s, k] for k in range(nodes) for s in range(3)], rows_ref, cols_ref
+    )
     chosen = [(s, o) for o in (1, 2, 3) for s in range(6 - o, 6)]
-    pairs = [cross(kept_ref[0, s - 3], ahead[s + o - 6]) for s, o in chosen]
-    place = [8 * (o - 1) + s for s, o in chosen]
-    row = lax.broadcasted_iota(jnp.int32, (24, LANES), 0)
-    mine = functools.reduce(jnp.logical_or, [row == p for p in place])
-    lane = lax.broadcasted_iota(jnp.int32, (24, LANES), 1)
-    by_rows, by_cols = moments(pairs, back_ref, weigh_ref, place)
-    old = measured_ref[...]
-    new = jnp.where(mine & (lane == node), by_rows, old)
-    measured_ref[...] = jnp.where(mine & (lane == node + HALF), by_cols, new)
-
-    @pl.when(node == pl.num_programs(0) - 1)
+    pairs = []
+    for k in range(nodes):
+        ahead = [spec[FULL * (3 * k + s) : FULL * (3 * k + s) + FULL] for s in range(3)]
+        pairs += [cross(kept_ref[k, s - 3], ahead[s + o - 6]) for s, o in chosen]
+    measured_ref[...] = put_shifts(
+        measured_ref[...], step, nodes, pairs, back_ref, weigh_ref, [8 * (o - 1) + s for s, o in chosen]
+    )
+
+    @pl.when(step == pl.num_programs(0) - 1)
     def _():
         measured = measured_ref[...] * weights_ref[...]
         measured_ref[...] = measured
@@ -236,9 +256,12 @@
     params = pltpu.CompilerParams(vmem_limit_bytes=48 * 1024 * 1024)
     own, kept = pl.pallas_call(
         own_kernel,
-        grid=(count,),
-        in_specs=[pl.BlockSpec((local, 1, LENGTH, LENGTH), lambda n: (0, n, 0, 0)), *table_specs],
-        out_specs=[whole, pl.BlockSpec((1, 3, FULL, 2 * LANES), lambda n: (n, 0, 0, 0))],
+        grid=(count // OWN_NODES,),
+        in_specs=[
+            pl.BlockSpec((local, OWN_NODES, LENGTH, LENGTH), lambda n: (0, n, 0, 0)),
+            *table_specs,
+        ],
+        out_specs=[whole, pl.BlockSpec((OWN_NODES, 3, FULL, 2 * LANES), lambda n: (n, 0, 0, 0))],
         out_shape=[
             jax.ShapeDtypeStruct((24, LANES), jnp.float32),
             jax.ShapeDtypeStruct((count, 3, FULL, 2 * LANES), jnp.bfloat16),
@@ -265,11 +288,11 @@
     smem = pl.BlockSpec(memory_space=pltpu.SMEM)
     measured_rows, message = pl.pallas_call(
         next_kernel,
-        grid=(count,),
+        grid=(count // NEXT_NODES,),
         in_specs=[
             smem,
-            pl.BlockSpec((reach, 1, LENGTH, LENGTH), lambda n: (0, n, 0, 0)),
-            pl.BlockSpec((1, 3, FULL, 2 * LANES), lambda n: (n, 0, 0, 0)),
+            pl.BlockSpec((reach, NEXT_NODES, LENGTH, LENGTH), lambda n: (0, n, 0, 0)),
+            pl.BlockSpec((NEXT_NODES, 3, FULL, 2 * LANES), lambda n: (n, 0, 0, 0)),
             *table_specs,
             whole,
             whole,

time: 73.1 us -> 62.2 us (0.85)
  the two profiles are of different devices: /device:TPU:8 before, /device:TPU:1 now
where the time goes in v2:
time: 62.2 us; the launch traced here: 61.9 us
  starting transfers between devices  19.6 us (32%)
  waiting for transfers between devices  18.4 us (30%)
  Pallas kernels  13.8 us (22%)
  local copies, waits for them, and re-layouts  8.68 us (14%)
  other arithmetic  0.77 us (1%)
  between operations  0.74 us (1%)
    ppermute x7, starting transfers between devices, turned_by(): lax.ppermute(value, axis, [(i, (i + by) % count) for i in range(count)])  14.4 us
    ppermute x7, waiting for transfers between devices, turned_by(): lax.ppermute(value, axis, [(i, (i + by) % count) for i in range(count)])  10.7 us
    ppermute x1, waiting for transfers between devices, shifted(): return lax.ppermute(value, axis, pairs)  7.68 us
    pallas_call x1, Pallas kernels, shards(): pl.pallas_call(own_kernel, grid=(count // OWN_NODES,), in_specs=[pl.Block...  6.58 us
    ppermute x1, starting transfers between devices, shifted(): return lax.ppermute(value, axis, pairs)  5.14 us
    pallas_call x1, Pallas kernels, shards(): pl.pallas_call(next_kernel, grid=(count // NEXT_NODES,), in_specs=[smem,...  4.82 us
    unnamed x22, local copies, waits for them, and re-layouts  3.68 us
    slice x1, local copies, waits for them, and re-layouts, shards(): received = shifted(flat[:reach], 'sec', -1)  2.91 us
  transfers between devices with their start and end apart: 8, of which 6 were waited for; matrix products, arithmetic and copies ran while one was open for 4% of the time, Pallas kernels for 11%

profile of v2, /device:TPU:1, one launch (start us, length us, event | category | flops | bytes accessed | tf_op | source)
XLA Modules:
  0.0 61.9 jit_solution(10699486252326108065)
XLA Ops:
  0.6 0.0 copy-start.6
  0.6 0.0 copy-start.5
  0.7 0.0 copy-start
  0.7 2.9 %slice.12 = bf16[3,2,8,128,128]{4,3,2,1,0:T(8,128)(2,1)} slice(bf16[6,2,8,128,128]{4,3,2,1,0:T(8,128)(2,1)} %param.7), slice={[0:3], [0:2], [0:8], [0:128], [0:128]} | slice | bytes 3145728 | tf_op jit(solution)/shard_map/slice | solution.py:253
  3.6 5.1 %collective-permute-start = (bf16[3,16,128,128]{3,2,1,0:T(8,128)(2,1)}, bf16[3,16,128,128]{3,2,1,0:T(8,128)(2,1)}, u32[]{:S(2)}, u32[]{:S(2)}) collective-permute-start(bf16[3,16,128,128]{3,2,1,0:T(8,128)(2,1)} %bitcast.1), channel_id=1, source_target_pairs={{4,0},{8,4},{12,8},{16,12},{20,16},{24,20},{28,24},{32,28},{36,32}... | collective-permute-start | bytes 4718600 | tf_op jit(solution)/shard_map/ppermute | solution.py:239
  8.8 0.8 %select_bitcast_fusion = f32[3,6]{1,0:T(4,128)S(1)} fusion(s32[6,3]{0,1:T(4,128)} %param.8, s32[3]{0:T(128)S(1)} %iota_add_fusion, s32[6]{0:T(128)S(1)} %iota_add_fusion.1), kind=kLoop, calls=%fused_computation.4 | loop fusion | flops 72 | bytes 180 | tf_op jit(solution)/shard_map/transpose | solution.py:281
  9.5 0.1 broadcast_in_dim.4
  9.6 0.8 %reshape.49 = f32[6,2,16]{2,0,1:T(8,128)S(1)} reshape(f32[6,2,2,8]{3,2,0,1:T(2,128)} %bitcast.23) | data formatting | bytes 1536 | tf_op jit(solution)/shard_map/reshape | solution.py:284
  10.4 0.1 reshape.44.nodes_ref
  10.5 0.0 copy-done.6
  10.5 0.0 copy-done.5
  10.5 0.0 copy-done
  10.5 0.0 copy-start.1
  10.5 0.9 %copy-done.1 = bf16[256,256]{1,0:T(8,128)(2,1)S(1)} copy-done((bf16[256,256]{1,0:T(8,128)(2,1)S(1)}, bf16[256,256]{1,0:T(8,128)(2,1)}, u32[]{:S(2)}) %copy-start.1) | copy-done | bytes 131096
  11.4 0.0 copy-start.3
  11.4 0.9 %copy-done.3 = bf16[256,256]{1,0:T(8,128)(2,1)S(1)} copy-done((bf16[256,256]{1,0:T(8,128)(2,1)S(1)}, bf16[256,256]{1,0:T(8,128)(2,1)}, u32[]{:S(2)}) %copy-start.3) | copy-done | bytes 131096
  12.3 0.0 copy-start.2
  12.3 0.0 copy-start.4
  12.3 6.6 %own_pairs.1 = (f32[24,128]{1,0:T(8,128)S(1)}, bf16[16,3,80,256]{3,2,1,0:T(8,128)(2,1)S(1)}) custom-call(bf16[6,16,128,128]{3,2,1,0:T(8,128)(2,1)S(1)} %bitcast.19, bf16[144,128]{1,0:T(8,128)(2,1)S(1)} %copy-done.5, bf16[256,256]{1,0:T(8,128)(2,1)S(1)} %copy-done.3, bf16[256,256]{1,0:T(8,128)(2,1)S(1)} %copy-done.1, bf16[80,128]{1,0:T(8,128)(2,1)S(1)} %copy-done.6), custom_call_target="tpu_custom_call" | custom-call | flops 8000000000 | bytes 6000000 | tf_op jit(solution)/shard_map/own_pairs/pallas_call | solution.py:257
  18.9 7.7 %collective-permute-done.patches_ref = bf16[3,16,128,128]{3,2,1,0:T(8,128)(2,1)} collective-permute-done((bf16[3,16,128,128]{3,2,1,0:T(8,128)(2,1)}, bf16[3,16,128,128]{3,2,1,0:T(8,128)(2,1)}, u32[]{:S(2)}, u32[]{:S(2)}) %collective-permute-start) | collective-permute-done | bytes 1572896 | tf_op jit(solution)/shard_map/ppermute | solution.py:239
  26.6 0.1 broadcast_in_dim.5.weights_ref
  26.6 0.0 copy-done.2
  26.6 0.0 copy-done.4
  26.6 4.8 %next_pairs.1 = (f32[24,128]{1,0:T(8,128)S(1)}, f32[32,128]{1,0:T(8,128)S(1)}) custom-call(s32[1]{0:T(128)} %bitcast.tile_ref, bf16[3,16,128,128]{3,2,1,0:T(8,128)(2,1)} %collective-permute-done.patches_ref, bf16[16,3,80,256]{3,2,1,0:T(8,128)(2,1)S(1)} %get-tuple-element.6.kept_ref, bf16[144,128]{1,0:T(8,128)(2,1)S(1)} %copy-done.5, ...), custom_call_target="tpu_custom_call" | custom-call | flops 4000000000 | bytes 4000000 | tf_op jit(solution)/shard_map/next_pairs/pallas_call | solution.py:289
  31.5 2.7 %collective-permute-start.3 = (f32[32,128]{1,0:T(8,128)S(1)}, f32[32,128]{1,0:T(8,128)S(1)}, u32[]{:S(2)}, u32[]{:S(2)}) collective-permute-start(f32[32,128]{1,0:T(8,128)S(1)} %get-tuple-element.8), channel_id=1, source_target_pairs={{0,3},{1,0},{2,1},{3,2},{4,7},{5,4},{6,5},{7,6},{8,11},{9,8},{10,9... | collective-permute-start | bytes 49160 | tf_op jit(solution)/shard_map/ppermute | solution.py:244
  34.2 0.4 collective-permute-start.2
  34.5 0.8 %collective-permute-start.1 = (f32[32,128]{1,0:T(8,128)S(1)}, f32[32,128]{1,0:T(8,128)S(1)}, u32[]{:S(2)}, u32[]{:S(2)}) collective-permute-start(f32[32,128]{1,0:T(8,128)S(1)} %get-tuple-element.8), channel_id=1, source_target_pairs={{0,1},{1,2},{2,3},{3,0},{4,5},{5,6},{6,7},{7,4},{8,9},{9,10},{10,1... | collective-permute-start | bytes 49160 | tf_op jit(solution)/shard_map/ppermute | solution.py:244
  35.3 0.0 collective-permute-done.3
  35.3 3.0 %collective-permute-done.2 = f32[32,128]{1,0:T(8,128)S(1)} collective-permute-done((f32[32,128]{1,0:T(8,128)S(1)}, f32[32,128]{1,0:T(8,128)S(1)}, u32[]{:S(2)}, u32[]{:S(2)}) %collective-permute-start.2) | collective-permute-done | bytes 16416 | tf_op jit(solution)/shard_map/ppermute | solution.py:244
  38.3 0.2 collective-permute-done.1
  38.5 0.0 collective-permute-start.5
  38.5 1.7 %collective-permute-start.4 = (f32[32,128]{1,0:T(8,128)S(1)}, f32[32,128]{1,0:T(8,128)S(1)}, u32[]{:S(2)}, u32[]{:S(2)}) collective-permute-start(f32[32,128]{1,0:T(8,128)S(1)} %add_add_fusion), channel_id=1, source_target_pairs={{0,4},{4,8},{8,12},{12,16},{16,20},{20,24},{24,28},{28,32},{32,36}... | collective-permute-start | bytes 49160 | tf_op jit(solution)/shard_map/ppermute | solution.py:244
  40.2 0.1 reshape.47
  40.3 1.3 %collective-permute-done.5 = f32[32,128]{1,0:T(8,128)S(1)} collective-permute-done((f32[32,128]{1,0:T(8,128)S(1)}, f32[32,128]{1,0:T(8,128)S(1)}, u32[]{:S(2)}, u32[]{:S(2)}) %collective-permute-start.5) | collective-permute-done | bytes 16416 | tf_op jit(solution)/shard_map/ppermute | solution.py:244
  41.7 0.0 collective-permute-done.4
  41.7 0.0 copy-start.7
  41.7 8.8 %collective-permute-start.7 = (f32[3,32,128]{2,1,0:T(8,128)S(1)}, f32[3,32,128]{2,1,0:T(8,128)S(1)}, u32[]{:S(2)}, u32[]{:S(2)}) collective-permute-start(f32[3,32,128]{2,1,0:T(8,128)S(1)} %pad_maximum_fusion.near_ref), channel_id=1, source_target_pairs={{0,244},{4,248},{8,252},{12,0},{16,4},{20,8},{24,12},{28,16},{32,2... | collective-permute-start | bytes 147464 | tf_op jit(solution)/shard_map/ppermute | solution.py:244
  50.5 0.0 collective-permute-start.6
  50.5 0.1 reshape.48
  50.6 0.6 %copy.15 = f32[2,6,3,2,8]{4,3,2,1,0:T(2,128)} copy(f32[2,6,3,2,8]{4,3,0,2,1:T(2,128)S(1)} %reshape.48) | data formatting | bytes 4608
  51.2 0.6 %collective-permute-done.7.high_ref = f32[3,32,128]{2,1,0:T(8,128)S(1)} collective-permute-done((f32[3,32,128]{2,1,0:T(8,128)S(1)}, f32[3,32,128]{2,1,0:T(8,128)S(1)}, u32[]{:S(2)}, u32[]{:S(2)}) %collective-permute-start.7) | collective-permute-done | bytes 49184 | tf_op jit(solution)/shard_map/ppermute | solution.py:244
  51.9 0.0 copy-start.8
  51.9 5.6 %collective-permute-done.6.low_ref = f32[3,32,128]{2,1,0:T(8,128)S(1)} collective-permute-done((f32[3,32,128]{2,1,0:T(8,128)S(1)}, f32[3,32,128]{2,1,0:T(8,128)S(1)}, u32[]{:S(2)}, u32[]{:S(2)}) %collective-permute-start.6) | collective-permute-done | bytes 49184 | tf_op jit(solution)/shard_map/ppermute | solution.py:244
  57.5 0.0 copy-done.7
  57.5 0.0 copy-done.8
  57.5 0.0 copy-start.9
  57.5 0.6 copy-done.9
  58.1 2.4 %relax.1 = f32[8,128]{1,0:T(8,128)} custom-call(s32[1]{0:T(128)} %bitcast.tile_ref, f32[3,32,128]{2,1,0:T(8,128)} %copy-done.7, f32[3,32,128]{2,1,0:T(8,128)} %copy-done.9, f32[3,32,128]{2,1,0:T(8,128)} %copy-done.8), custom_call_target="tpu_custom_call" | custom-call | tf_op jit(solution)/shard_map/relax/pallas_call | solution.py:317
  60.4 0.8 %reshape.45 = f32[8,2,64]{2,1,0:T(2,128)S(1)} reshape(f32[8,128]{1,0:T(8,128)} %relax.1) | data formatting | bytes 8192 | tf_op jit(solution)/shard_map/reshape | solution.py:330
  61.2 0.1 reshape.46
  61.3 0.6 copy.14
  (9 shorter events, 0.1 us)
Async XLA Ops:
  0.6 9.9 %copy-start.6 = (bf16[80,128]{1,0:T(8,128)(2,1)S(1)}, bf16[80,128]{1,0:T(8,128)(2,1)}, u32[]{:S(2)}) copy-start(bf16[80,128]{1,0:T(8,128)(2,1)} %constant.30.clone.weigh_ref) | copy-start | bytes 61444
  0.6 9.8 %copy-start.5 = (bf16[144,128]{1,0:T(8,128)(2,1)S(1)}, bf16[144,128]{1,0:T(8,128)(2,1)}, u32[]{:S(2)}) copy-start(bf16[144,128]{1,0:T(8,128)(2,1)} %constant.27.clone.rows_ref) | copy-start | bytes 110596
  0.7 9.8 %copy-start = (bf16[6,2,8,128,128]{4,3,2,1,0:T(8,128)(2,1)S(1)}, bf16[6,2,8,128,128]{4,3,2,1,0:T(8,128)(2,1)}, u32[]{:S(2)}) copy-start(bf16[6,2,8,128,128]{4,3,2,1,0:T(8,128)(2,1)} %param.7) | copy-start | bytes 9437188
  3.6 23.0 %collective-permute-start = (bf16[3,16,128,128]{3,2,1,0:T(8,128)(2,1)}, bf16[3,16,128,128]{3,2,1,0:T(8,128)(2,1)}, u32[]{:S(2)}, u32[]{:S(2)}) collective-permute-start(bf16[3,16,128,128]{3,2,1,0:T(8,128)(2,1)} %bitcast.1), channel_id=1, source_target_pairs={{4,0},{8,4},{12,8},{16,12},{20,16},{24,20},{28,24},{32,28},{36,32}... | collective-permute-start | bytes 4718600 | tf_op jit(solution)/shard_map/ppermute | solution.py:239
  10.5 0.9 %copy-start.1 = (bf16[256,256]{1,0:T(8,128)(2,1)S(1)}, bf16[256,256]{1,0:T(8,128)(2,1)}, u32[]{:S(2)}) copy-start(bf16[256,256]{1,0:T(8,128)(2,1)} %constant.29.clone.back_ref) | copy-start | bytes 393220
  11.4 0.9 %copy-start.3 = (bf16[256,256]{1,0:T(8,128)(2,1)S(1)}, bf16[256,256]{1,0:T(8,128)(2,1)}, u32[]{:S(2)}) copy-start(bf16[256,256]{1,0:T(8,128)(2,1)} %constant.28.clone.cols_ref) | copy-start | bytes 393220
  12.3 14.3 %copy-start.2 = (bf16[256,256]{1,0:T(8,128)(2,1)S(1)}, bf16[256,256]{1,0:T(8,128)(2,1)}, u32[]{:S(2)}) copy-start(bf16[256,256]{1,0:T(8,128)(2,1)} %constant.29.clone.back_ref) | copy-start | bytes 393220
  12.3 14.3 %copy-start.4 = (bf16[256,256]{1,0:T(8,128)(2,1)S(1)}, bf16[256,256]{1,0:T(8,128)(2,1)}, u32[]{:S(2)}) copy-start(bf16[256,256]{1,0:T(8,128)(2,1)} %constant.28.clone.cols_ref) | copy-start | bytes 393220
  31.5 3.8 %collective-permute-start.3 = (f32[32,128]{1,0:T(8,128)S(1)}, f32[32,128]{1,0:T(8,128)S(1)}, u32[]{:S(2)}, u32[]{:S(2)}) collective-permute-start(f32[32,128]{1,0:T(8,128)S(1)} %get-tuple-element.8), channel_id=1, source_target_pairs={{0,3},{1,0},{2,1},{3,2},{4,7},{5,4},{6,5},{7,6},{8,11},{9,8},{10,9... | collective-permute-start | bytes 49160 | tf_op jit(solution)/shard_map/ppermute | solution.py:244
  34.2 4.1 %collective-permute-start.2 = (f32[32,128]{1,0:T(8,128)S(1)}, f32[32,128]{1,0:T(8,128)S(1)}, u32[]{:S(2)}, u32[]{:S(2)}) collective-permute-start(f32[32,128]{1,0:T(8,128)S(1)} %get-tuple-element.8), channel_id=1, source_target_pairs={{0,2},{1,3},{2,0},{3,1},{4,6},{5,7},{6,4},{7,5},{8,10},{9,11},{10,... | collective-permute-start | bytes 49160 | tf_op jit(solution)/shard_map/ppermute | solution.py:244
  34.5 3.9 %collective-permute-start.1 = (f32[32,128]{1,0:T(8,128)S(1)}, f32[32,128]{1,0:T(8,128)S(1)}, u32[]{:S(2)}, u32[]{:S(2)}) collective-permute-start(f32[32,128]{1,0:T(8,128)S(1)} %get-tuple-element.8), channel_id=1, source_target_pairs={{0,1},{1,2},{2,3},{3,0},{4,5},{5,6},{6,7},{7,4},{8,9},{9,10},{10,1... | collective-permute-start | bytes 49160 | tf_op jit(solution)/shard_map/ppermute | solution.py:244
  38.5 3.2 %collective-permute-start.5 = (f32[32,128]{1,0:T(8,128)S(1)}, f32[32,128]{1,0:T(8,128)S(1)}, u32[]{:S(2)}, u32[]{:S(2)}) collective-permute-start(f32[32,128]{1,0:T(8,128)S(1)} %add_add_fusion), channel_id=1, source_target_pairs={{0,252},{4,0},{8,4},{12,8},{16,12},{20,16},{24,20},{28,24},{32,28}... | collective-permute-start | bytes 49160 | tf_op jit(solution)/shard_map/ppermute | solution.py:244
  38.5 3.2 %collective-permute-start.4 = (f32[32,128]{1,0:T(8,128)S(1)}, f32[32,128]{1,0:T(8,128)S(1)}, u32[]{:S(2)}, u32[]{:S(2)}) collective-permute-start(f32[32,128]{1,0:T(8,128)S(1)} %add_add_fusion), channel_id=1, source_target_pairs={{0,4},{4,8},{8,12},{12,16},{16,20},{20,24},{24,28},{28,32},{32,36}... | collective-permute-start | bytes 49160 | tf_op jit(solution)/shard_map/ppermute | solution.py:244
  41.7 15.8 %copy-start.7 = (f32[3,32,128]{2,1,0:T(8,128)}, f32[3,32,128]{2,1,0:T(8,128)S(1)}, u32[]{:S(2)}) copy-start(f32[3,32,128]{2,1,0:T(8,128)S(1)} %pad_maximum_fusion.near_ref) | copy-start | bytes 147460
  41.7 10.2 %collective-permute-start.7 = (f32[3,32,128]{2,1,0:T(8,128)S(1)}, f32[3,32,128]{2,1,0:T(8,128)S(1)}, u32[]{:S(2)}, u32[]{:S(2)}) collective-permute-start(f32[3,32,128]{2,1,0:T(8,128)S(1)} %pad_maximum_fusion.near_ref), channel_id=1, source_target_pairs={{0,244},{4,248},{8,252},{12,0},{16,4},{20,8},{24,12},{28,16},{32,2... | collective-permute-start | bytes 147464 | tf_op jit(solution)/shard_map/ppermute | solution.py:244
  50.5 7.0 %collective-permute-start.6 = (f32[3,32,128]{2,1,0:T(8,128)S(1)}, f32[3,32,128]{2,1,0:T(8,128)S(1)}, u32[]{:S(2)}, u32[]{:S(2)}) collective-permute-start(f32[3,32,128]{2,1,0:T(8,128)S(1)} %pad_maximum_fusion.near_ref), channel_id=1, source_target_pairs={{0,12},{4,16},{8,20},{12,24},{16,28},{20,32},{24,36},{28,40},{32,4... | collective-permute-start | bytes 147464 | tf_op jit(solution)/shard_map/ppermute | solution.py:244
  51.9 5.6 %copy-start.8 = (f32[3,32,128]{2,1,0:T(8,128)}, f32[3,32,128]{2,1,0:T(8,128)S(1)}, u32[]{:S(2)}) copy-start(f32[3,32,128]{2,1,0:T(8,128)S(1)} %collective-permute-done.7.high_ref) | copy-start | bytes 147460
  57.5 0.6 copy-start.9

commit v3 on v2

v3 whole, which is shorter than its diff:
```python
import functools

import jax
import jax.numpy as jnp
import ml_dtypes
import numpy as np
from jax import lax
from jax.experimental import pallas as pl
from jax.experimental.pallas import tpu as pltpu
from jax.sharding import PartitionSpec as P

SWEEPS = 8
STEP_SIZE = 0.08
EPSILON = 1e-06
LENGTH = 128
HALF = 64
LANES = 128
PACKS = 3
PACK_VMEM = 8
PACK_OUT = pl.BlockSpec(memory_space=pl.ANY)
OWN_VMEM = 48
BORDER_VMEM = 48
KEPT = 5
FULL = 80


def tables():
    index = np.arange(LENGTH)
    phase = (index[:, None] * index[None, :] % LENGTH) * (2.0 * np.pi / LENGTH)
    cosine, sine = np.cos(phase), np.sin(phase)
    shifts = np.where(index < HALF, index, index - LENGTH).astype(np.float64)
    rows = np.zeros((144, LENGTH))
    rows[:HALF] = cosine[:HALF]
    rows[HALF:LENGTH] = sine[:HALF]
    rows[LENGTH] = cosine[HALF]
    cols = np.block([[cosine, -sine], [-sine, -cosine]])
    back = np.block([[cosine, sine], [-sine, cosine]])
    basis = np.concatenate([2.0 * cosine[:, :HALF], -2.0 * sine[:, :HALF]], axis=1)
    basis[:, 0] = 1.0
    basis[:, HALF] = cosine[:, HALF]
    form = basis.T @ (shifts[:, None] * basis)
    cos_part = np.arange(LENGTH) <= HALF
    half_form = np.where(cos_part[None, :], form, 2.0 * form)
    weigh = np.zeros((FULL, LENGTH))
    weigh[: HALF + 1] = half_form[: HALF + 1]
    weigh = np.where(np.abs(weigh) < 1e-6, 0.0, weigh)
    top = np.zeros((144, 2 * LANES))
    top[:, :LANES] = rows
    top[:FULL, LANES:] = weigh
    return np.concatenate([top, cols, back], axis=0).astype(ml_dtypes.bfloat16)


def dot(a, b):
    return lax.dot_general(a, b, (((1,), (0,)), ((), ())), preferred_element_type=jnp.float32)


def spectra(patches, tabs_ref):
    part = dot(tabs_ref[:144, :LANES], jnp.concatenate(patches, axis=1)).astype(jnp.bfloat16)
    stacked = []
    for s in range(len(patches)):
        lanes = slice(s * LANES, (s + 1) * LANES)
        stacked.append(jnp.concatenate([part[:HALF, lanes], part[HALF:LENGTH, lanes]], axis=1))
        stacked.append(
            jnp.concatenate([part[LENGTH:, lanes], jnp.zeros((16, LANES), jnp.bfloat16)], axis=1)
        )
    return dot(jnp.concatenate(stacked, axis=0), tabs_ref[144:400]).astype(jnp.bfloat16)


def cross(a, b, sign=None):
    a = a[:72].astype(jnp.float32)
    b = b[:72].astype(jnp.float32)
    ar, ai = a[:, :LANES], a[:, LANES:]
    br, bi = b[:, :LANES], b[:, LANES:]
    real = ar * br + ai * bi
    imag = ar * bi - ai * br
    if sign is not None:
        imag = imag * sign
    top_real = real[:8] - imag[HALF:]
    top_imag = imag[:8] + real[HALF:]
    real = jnp.concatenate([top_real, real[8:HALF]], axis=0)
    imag = jnp.concatenate([top_imag, imag[8:HALF]], axis=0)
    return jnp.concatenate([real, imag], axis=1).astype(jnp.bfloat16)


def tile_sum(values):
    total = values[0:8]
    for v in range(1, HALF // 8):
        total = total + values[8 * v : 8 * v + 8]
    return total


def moments(pairs, tabs_ref):
    count = len(pairs)
    back = dot(jnp.concatenate(pairs, axis=0), tabs_ref[400:])
    reals = [back[HALF * n : HALF * n + HALF, :LANES] for n in range(count)]
    imags = [back[HALF * n : HALF * n + HALF, LANES:] for n in range(count)]
    stacked = jnp.concatenate(
        [jnp.concatenate([r, i], axis=0).astype(jnp.bfloat16) for r, i in zip(reals, imags)], axis=1
    )
    weighed = dot(tabs_ref[:FULL, LANES:], stacked)
    first = lax.broadcasted_iota(jnp.int32, (8, LANES), 0) == 0
    powers, alongs = [], []
    for n in range(count):
        real, imag = reals[n], imags[n]
        square = real * real + imag * imag
        power = 2.0 * tile_sum(square) - jnp.where(first, square[:8], 0.0)
        lanes = slice(n * LANES, (n + 1) * LANES)
        along = tile_sum(real * weighed[:HALF, lanes]) + imag[:8] * weighed[HALF:72, lanes]
        powers.append(jnp.sum(power, axis=0, keepdims=True))
        alongs.append(jnp.sum(along, axis=0, keepdims=True))
    return powers, alongs


def shifts_of(powers, alongs, places):
    zero = jnp.zeros((1, LANES), jnp.float32)
    at = dict(zip(places, range(len(places))))
    power = jnp.concatenate([powers[at[r]] if r in at else zero for r in range(24)], axis=0)
    along = jnp.concatenate([alongs[at[r]] if r in at else zero for r in range(24)], axis=0)
    place = lax.broadcasted_iota(jnp.int32, (24, LANES), 1)
    shift = jnp.where(place < HALF, place, place - LENGTH).astype(jnp.float32)
    total = jnp.sum(power, axis=1, keepdims=True) * 2.0**-49 + EPSILON
    by_rows = jnp.sum(along, axis=1, keepdims=True) * 2.0**-56
    by_cols = jnp.sum(power * shift, axis=1, keepdims=True) * 2.0**-49
    return by_rows / total, by_cols / total


def put_shifts(acc, step, nodes, pairs, tabs_ref, places):
    powers, alongs = moments(pairs, tabs_ref)
    lane = lax.broadcasted_iota(jnp.int32, (24, LANES), 1)
    each = len(places)
    for k in range(nodes):
        mine = slice(k * each, (k + 1) * each)
        by_rows, by_cols = shifts_of(powers[mine], alongs[mine], places)
        node = step * nodes + k
        here = jnp.where(lane == node, by_rows, jnp.where(lane == node + HALF, by_cols, 0.0))
        acc = acc + here
    return acc


def pack_kernel(patches_ref, first_ref, last_ref, sems):
    count = first_ref.shape[0]
    begin = patches_ref.shape[0] - count
    each = count // PACKS
    copies = []
    for n in range(2 * PACKS):
        out_ref, at = (first_ref, n * each) if n < PACKS else (last_ref, (n - PACKS) * each)
        source = at if n < PACKS else begin + at
        copies.append(
            pltpu.make_async_copy(
                patches_ref.at[pl.ds(source, each)], out_ref.at[pl.ds(at, each)], sems.at[n]
            )
        )
    for copy in copies:
        copy.start()
    for copy in copies:
        copy.wait()


def own_kernel(patches_ref, tabs_ref, acc_ref, kept_ref):
    step = pl.program_id(0)
    nodes = patches_ref.shape[1]

    @pl.when(step == 0)
    def _():
        acc_ref[...] = jnp.zeros_like(acc_ref)

    spec = spectra([patches_ref[s, k] for k in range(nodes) for s in range(6)], tabs_ref)
    chosen = [(s, o) for o in (1, 2, 3) for s in range(6 - o)]
    pairs = []
    for k in range(nodes):
        specs = [spec[FULL * (6 * k + s) : FULL * (6 * k + s) + FULL] for s in range(6)]
        for s in range(KEPT):
            kept_ref[k, s] = specs[1 + s]
        pairs += [cross(specs[s], specs[s + o]) for s, o in chosen]
    acc_ref[...] = put_shifts(
        acc_ref[...], step, nodes, pairs, tabs_ref, [8 * (o - 1) + s for s, o in chosen]
    )


def next_kernel(
    place_ref, right_ref, right_more_ref, left_ref, left_more_ref, kept_ref, tabs_ref,
    own_ref, flags_ref, nodes_ref, message_ref, acc_ref, *, sections,
):
    step = pl.program_id(0)
    nodes = right_ref.shape[0]

    @pl.when(step == 0)
    def _():
        acc_ref[...] = own_ref[...]

    early = step == 0
    sign = jnp.where(early, -1.0, 1.0).astype(jnp.float32)
    mate = jnp.where(early, 3, 0)
    inputs = []
    for k in range(nodes):
        third = jnp.where(early, right_more_ref[k], left_more_ref[k])
        inputs += [right_ref[k], left_ref[k], third]
    spec = spectra(inputs, tabs_ref)
    pairs = []
    for k in range(nodes):
        six, before, third = [spec[FULL * (3 * k + s) : FULL * (3 * k + s) + FULL] for s in range(3)]
        pairs += [cross(kept_ref[k, s - 1], six) for s in (5, 4, 3)]
        pairs += [cross(before, kept_ref[k, s - 1]) for s in (1, 2)]
        pairs.append(cross(third, kept_ref[k, mate], sign))
    acc = put_shifts(acc_ref[...], step, nodes, pairs, tabs_ref, [5, 12, 19, 14, 22, 23])
    lane = lax.broadcasted_iota(jnp.int32, (24, LANES), 1)
    row = lax.broadcasted_iota(jnp.int32, (24, LANES), 0)
    own_third = lane % HALF < nodes
    moved = pltpu.roll(acc, 21, 0)
    acc = jnp.where((row == 20) & own_third & early, moved, acc)
    acc_ref[...] = jnp.where((row == 23) & own_third, 0.0, acc)

    @pl.when(step == pl.num_programs(0) - 1)
    def _():
        gap = jnp.zeros((6, HALF - 16), jnp.float32)
        u = jnp.concatenate(
            [nodes_ref[0, :, 0], nodes_ref[0, :, 1], gap, nodes_ref[1, :, 0], nodes_ref[1, :, 1], gap],
            axis=1,
        )
        flags = jnp.concatenate(
            [flags_ref[...].astype(jnp.float32), jnp.zeros((6, LANES - 3), jnp.float32)], axis=1
        )
        ahead = place_ref[1] * 6 + lax.broadcasted_iota(jnp.int32, (6, LANES), 0)
        ahead = ahead + 1 + lax.broadcasted_iota(jnp.int32, (6, LANES), 1)
        flags = jnp.where(ahead < sections, flags, 0.0)
        two = jnp.zeros((2, LANES), jnp.float32)
        message = jnp.concatenate([u, two, flags, two, acc_ref[...]], axis=0)
        message_ref[...] = pltpu.roll(message, place_ref[0] * 16, 1)


def relax_kernel(place_ref, near_ref, low_ref, high_ref, u_out, m_out, u_ref, w_ref, m_ref):
    u_ref[...] = jnp.zeros_like(u_ref)
    w_ref[...] = jnp.zeros_like(w_ref)
    m_ref[...] = jnp.zeros_like(m_ref)
    for trio, centre in ((low_ref, 1), (near_ref, 4), (high_ref, 7)):
        for part, by in ((0, 0), (1, -1), (2, 1)):
            row = 8 + 6 * (centre + by)
            u_ref[row : row + 6] = trio[part, 0:6]
            w_ref[row : row + 6] = trio[part, 8:14]
            for o in range(3):
                m_ref[o, row : row + 6] += trio[part, 16 + 8 * o : 22 + 8 * o]
            m_ref[1, row - 1 : row] += trio[part, 30:31]
            m_ref[2, row - 1 : row] += trio[part, 38:39]
            m_ref[2, row - 2 : row - 1] += trio[part, 39:40]
    u = u_ref[...]
    flags = w_ref[...]
    lane = lax.broadcasted_iota(jnp.int32, u.shape, 1)
    pull = jnp.zeros_like(u)
    weights = []
    for o in range(3):
        weight = jnp.sum(jnp.where(lane % 16 == o, flags, 0.0), axis=1, keepdims=True) * 0.25
        weight = jnp.broadcast_to(weight, u.shape)
        weights.append(weight)
        measured = m_ref[o] * weight
        m_ref[o] = measured
        pull = pull - measured + pltpu.roll(measured, o + 1, 0)
    col = lane % 8
    row = (lane // 8) % 8
    masks = [
        (m.astype(jnp.float32), by)
        for m, by in ((col > 0, 1), (col < 7, LANES - 1), (row > 0, 8), (row < 7, LANES - 8))
    ]
    degree = masks[0][0] + masks[1][0] + masks[2][0] + masks[3][0]
    for _ in range(SWEEPS):
        force = pull - degree * u
        for mask, by in masks:
            force = force + mask * pltpu.roll(u, by, 1)
        for o in (1, 2, 3):
            resid = weights[o - 1] * (pltpu.roll(u, u.shape[0] - o, 0) - u)
            force = force + resid - pltpu.roll(resid, o, 0)
        u = u + STEP_SIZE * force
    turn = lax.rem(LANES - place_ref[0] * 16, LANES)
    relaxed = pltpu.roll(u[32:40], turn, 1)
    for c in range(2):
        for i in range(2):
            lanes = slice(HALF * c + 8 * i, HALF * c + 8 * i + 8)
            u_out[c, :, i, :] = relaxed[:6, lanes]
    for o in range(3):
        measured = pltpu.roll(m_ref[o, 32:40], turn, 1)
        for c in range(2):
            for i in range(2):
                lanes = slice(HALF * c + 8 * i, HALF * c + 8 * i + 8)
                m_out[c, :, o, i, :] = measured[:6, lanes]


def shifted(value, axis, by):
    count = lax.axis_size(axis)
    pairs = [(i, i + by) for i in range(count) if 0 <= i + by < count]
    return lax.ppermute(value, axis, pairs)


def turned_by(value, axis, by):
    count = lax.axis_size(axis)
    return lax.ppermute(value, axis, [(i, (i + by) % count) for i in range(count)])


def shards(patches, pair_flags, nodes):
    local, rows_local, columns = patches.shape[:3]
    reach = pair_flags.shape[1]
    count = rows_local * columns
    step = count // 2
    sent = count + step
    sections = lax.axis_size("sec") * local
    tabs = tables()
    own_params = pltpu.CompilerParams(vmem_limit_bytes=OWN_VMEM * 1024 * 1024)
    border_params = pltpu.CompilerParams(vmem_limit_bytes=BORDER_VMEM * 1024 * 1024)
    anywhere = pl.BlockSpec(memory_space=pl.ANY)
    smem = pl.BlockSpec(memory_space=pltpu.SMEM)
    vmem = pl.BlockSpec(memory_space=pltpu.VMEM)

    def whole(*shape):
        return pl.BlockSpec(shape, lambda n: (0,) * len(shape))

    def block(at):
        return pl.BlockSpec((step, LENGTH, LENGTH), at)

    flat = patches.reshape(local * count, LENGTH, LENGTH)
    first, last = pl.pallas_call(
        pack_kernel,
        in_specs=[pl.BlockSpec(memory_space=pltpu.HBM)],
        out_specs=[PACK_OUT] * 2,
        out_shape=[jax.ShapeDtypeStruct((sent, LENGTH, LENGTH), patches.dtype)] * 2,
        scratch_shapes=[
            pltpu.SemaphoreType.DMA((2 * PACKS,)),
        ],
        compiler_params=pltpu.CompilerParams(vmem_limit_bytes=PACK_VMEM * 1024 * 1024),
        cost_estimate=pl.CostEstimate(flops=0, bytes_accessed=3_000_000, transcendentals=0),
        name="pack",
    )(flat)
    from_right = shifted(first, "sec", -1)
    from_left = shifted(last, "sec", 1)

    own, kept = pl.pallas_call(
        own_kernel,
        grid=(count // step,),
        in_specs=[
            pl.BlockSpec((local, step, LENGTH, LENGTH), lambda n: (0, n, 0, 0)),
            whole(*tabs.shape),
        ],
        out_specs=[
            whole(24, LANES),
            pl.BlockSpec((step, KEPT, FULL, 2 * LANES), lambda n: (n, 0, 0, 0)),
        ],
        out_shape=[
            jax.ShapeDtypeStruct((24, LANES), jnp.float32),
            jax.ShapeDtypeStruct((count, KEPT, FULL, 2 * LANES), jnp.bfloat16),
        ],
        compiler_params=own_params,
        cost_estimate=pl.CostEstimate(flops=8_000_000_000, bytes_accessed=6_000_000, transcendentals=0),
        name="own_pairs",
    )(patches.reshape(local, count, LENGTH, LENGTH), tabs)

    place = jnp.stack([lax.axis_index("tile"), lax.axis_index("sec")]).astype(jnp.int32)
    message = pl.pallas_call(
        functools.partial(next_kernel, sections=sections),
        grid=(count // step,),
        in_specs=[
            smem,
            block(lambda n: (n, 0, 0)),
            block(lambda n: (2, 0, 0)),
            block(lambda n: (n + 1, 0, 0)),
            block(lambda n: (0, 0, 0)),
            pl.BlockSpec((step, KEPT, FULL, 2 * LANES), lambda n: (n, 0, 0, 0)),
            whole(*tabs.shape),
            whole(24, LANES),
            whole(*pair_flags.shape),
            whole(*nodes.shape),
        ],
        out_specs=whole(40, LANES),
        out_shape=jax.ShapeDtypeStruct((40, LANES), jnp.float32),
        scratch_shapes=[pltpu.VMEM((24, LANES), jnp.float32)],
        compiler_params=border_params,
        cost_estimate=pl.CostEstimate(flops=4_000_000_000, bytes_accessed=4_000_000, transcendentals=0),
        name="border_pairs",
    )(place, from_right, from_right, from_left, from_left, kept, tabs, own, pair_flags, nodes)

    joined = message
    for by in range(1, lax.axis_size("tile")):
        joined = joined + turned_by(message, "tile", by)
    near = jnp.stack([joined, turned_by(joined, "sec", 1), turned_by(joined, "sec", -1)], axis=0)
    low = turned_by(near, "sec", 3)
    high = turned_by(near, "sec", -3)
    return pl.pallas_call(
        relax_kernel,
        in_specs=[smem] + [vmem] * 3,
        out_specs=[vmem] * 2,
        out_shape=[
            jax.ShapeDtypeStruct(nodes.shape, jnp.float32),
            jax.ShapeDtypeStruct((2, local, reach, rows_local, columns), jnp.float32),
        ],
        scratch_shapes=[
            pltpu.VMEM((72, LANES), jnp.float32),
            pltpu.VMEM((72, LANES), jnp.float32),
            pltpu.VMEM((3, 72, LANES), jnp.float32),
        ],
        compiler_params=pltpu.CompilerParams(vmem_limit_bytes=8 * 1024 * 1024),
        name="relax",
    )(place, near, low, high)


def solution(mesh):
    placed = (P("sec", "tile", None, None, None), P("sec", None), P(None, "sec", "tile", None))
    return jax.shard_map(
        shards,
        mesh=mesh,
        in_specs=placed,
        out_specs=(P(None, "sec", "tile", None), P(None, "sec", None, "tile", None)),
        check_vma=False,
    )
```

time: 62.2 us -> 55.9 us (0.90)
  starting transfers between devices: 19.6 us -> 17 us
  waiting for transfers between devices: 18.4 us -> 16.2 us
  local copies, waits for them, and re-layouts: 8.68 us -> 7.44 us
  other arithmetic: 0.77 us -> 0.09 us
    ppermute x1 -> x2, waiting for transfers between devices: 7.68 us -> 0.01 us  [shifted(): return lax.ppermute(value, axis, pairs)]
    ppermute x7, waiting for transfers between devices: 10.7 us -> 16.2 us  [turned_by(): lax.ppermute(value, axis, [(i, (i + by) % count) for i in range(count)])]
    ppermute x7, starting transfers between devices: 14.4 us -> 9.97 us  [turned_by(): lax.ppermute(value, axis, [(i, (i + by) % count) for i in range(count)])]
    unnamed x22 -> x13, local copies, waits for them, and re-layouts: 3.68 us -> 7.44 us
    slice x1 -> x0, local copies, waits for them, and re-layouts: 2.91 us -> none  [shards(): received = shifted(flat[:reach], 'sec', -1)]
    ppermute x1 -> x2, starting transfers between devices: 5.14 us -> 7.07 us  [shifted(): return lax.ppermute(value, axis, pairs)]
    reshape x7 -> x0, local copies, waits for them, and re-layouts: 1.91 us -> none  [the longest x2 0.79 us: shards(): jnp.transpose(nodes, (1, 0, 2, 3)).reshape(local, 2, count)]
    transpose x1 -> x0, other arithmetic: 0.76 us -> none  [shards(): weight_rows = jnp.broadcast_to(jnp.pad(weights.T, ((0, 0), (0, 2)))[:, :,...]
  transfers between devices with their start and end apart: 8 -> 9, of which waited for: 6 -> 6; matrix products, arithmetic and copies ran while one was open for 4% -> 2% of each run, Pallas kernels for 11% -> 13%
where the time goes in v3:
time: 55.9 us; the launch traced here: 55.6 us
  starting transfers between devices  17 us (30%)
  waiting for transfers between devices  16.2 us (29%)
  Pallas kernels  14.1 us (25%)
  local copies, waits for them, and re-layouts  7.44 us (13%)
  between operations  0.7 us (1%)
    ppermute x7, waiting for transfers between devices, turned_by(): lax.ppermute(value, axis, [(i, (i + by) % count) for i in range(count)])  16.2 us
    ppermute x7, starting transfers between devices, turned_by(): lax.ppermute(value, axis, [(i, (i + by) % count) for i in range(count)])  9.97 us
    unnamed x13, local copies, waits for them, and re-layouts  7.44 us
    pallas_call x1, Pallas kernels, shards(): pl.pallas_call(own_kernel, grid=(count // step,), in_specs=[pl.BlockSpec(...  7.31 us
    ppermute x2, starting transfers between devices, shifted(): return lax.ppermute(value, axis, pairs)  7.07 us
    pallas_call x1, Pallas kernels, shards(): pl.pallas_call(functools.partial(next_kernel, sections=sections), grid=(c...  4.59 us
    pallas_call x1, Pallas kernels, shards(): pl.pallas_call(relax_kernel, in_specs=[smem] + [vmem] * 3, out_specs=[vme...  2.05 us
  transfers between devices with their start and end apart: 9, of which 6 were waited for; matrix products, arithmetic and copies ran while one was open for 2% of the time, Pallas kernels for 13%

profile of v3, /device:TPU:1, one launch (start us, length us, event | category | flops | bytes accessed | tf_op | source)
XLA Modules:
  0.0 55.6 jit_solution(4329833061731561475)
XLA Ops:
  0.6 0.0 copy-start
  0.6 1.9 %copy-done = bf16[6,2,8,128,128]{4,3,2,1,0:T(8,128)(2,1)S(1)} copy-done((bf16[6,2,8,128,128]{4,3,2,1,0:T(8,128)(2,1)S(1)}, bf16[6,2,8,128,128]{4,3,2,1,0:T(8,128)(2,1)}, u32[]{:S(2)}) %copy-start) | copy-done | bytes 3145752
  2.5 0.2 pack.1
  2.7 5.1 %collective-permute-start = (bf16[24,128,128]{2,1,0:T(8,128)(2,1)S(1)}, bf16[24,128,128]{2,1,0:T(8,128)(2,1)S(1)}, u32[]{:S(2)}, u32[]{:S(2)}) collective-permute-start(bf16[24,128,128]{2,1,0:T(8,128)(2,1)S(1)} %get-tuple-element.6), channel_id=1, source_target_pairs={{4,0},{8,4},{12,8},{16,12},{20,16},{24,20},{28,24},{32,28},{36,32}... | collective-permute-start | bytes 2359304 | tf_op jit(solution)/shard_map/ppermute | solution.py:289
  7.9 1.9 %collective-permute-start.1 = (bf16[24,128,128]{2,1,0:T(8,128)(2,1)S(1)}, bf16[24,128,128]{2,1,0:T(8,128)(2,1)S(1)}, u32[]{:S(2)}, u32[]{:S(2)}) collective-permute-start(bf16[24,128,128]{2,1,0:T(8,128)(2,1)S(1)} %get-tuple-element.7), channel_id=1, source_target_pairs={{0,4},{4,8},{8,12},{12,16},{16,20},{20,24},{24,28},{28,32},{32,36}... | collective-permute-start | bytes 2359304 | tf_op jit(solution)/shard_map/ppermute | solution.py:289
  9.8 0.1 pad_add_fusion.place_ref
  9.9 0.8 %copy.6.flags_ref = s32[6,3]{1,0:T(8,128)S(1)} copy(s32[6,3]{0,1:T(4,128)} %param.5) | data formatting | bytes 144 | tf_op args[1]
  10.6 0.0 copy-start.1
  10.6 1.9 %copy-done.1 = bf16[6,2,8,128,128]{4,3,2,1,0:T(8,128)(2,1)S(1)} copy-done((bf16[6,2,8,128,128]{4,3,2,1,0:T(8,128)(2,1)S(1)}, bf16[6,2,8,128,128]{4,3,2,1,0:T(8,128)(2,1)}, u32[]{:S(2)}) %copy-start.1) | copy-done | bytes 3145752
  12.5 0.0 copy-start.3
  12.5 1.0 %copy-done.3 = bf16[656,256]{1,0:T(8,128)(2,1)S(1)} copy-done((bf16[656,256]{1,0:T(8,128)(2,1)S(1)}, bf16[656,256]{1,0:T(8,128)(2,1)}, u32[]{:S(2)}) %copy-start.3) | copy-done | bytes 335896
  13.5 0.0 copy-start.2
  13.5 0.0 copy-start.4
  13.5 7.3 %own_pairs.1 = (f32[24,128]{1,0:T(8,128)S(1)}, bf16[16,5,80,256]{3,2,1,0:T(8,128)(2,1)}) custom-call(bf16[6,16,128,128]{3,2,1,0:T(8,128)(2,1)S(1)} %bitcast.8, bf16[656,256]{1,0:T(8,128)(2,1)S(1)} %copy-done.3), custom_call_target="tpu_custom_call" | custom-call | flops 8000000000 | bytes 6000000 | tf_op jit(solution)/shard_map/own_pairs/pallas_call | solution.py:333
  20.8 0.0 collective-permute-done.right_ref.right_more_ref
  20.8 0.0 collective-permute-done.1.left_ref.left_more_ref
  20.8 0.0 copy-done.2
  20.8 0.0 copy-done.4
  20.8 0.0 copy-start.5
  20.8 1.9 %copy-done.5 = bf16[16,5,80,256]{3,2,1,0:T(8,128)(2,1)S(1)} copy-done((bf16[16,5,80,256]{3,2,1,0:T(8,128)(2,1)S(1)}, bf16[16,5,80,256]{3,2,1,0:T(8,128)(2,1)}, u32[]{:S(2)}) %copy-start.5) | copy-done | bytes 3276824
  22.8 4.6 %border_pairs.1 = f32[40,128]{1,0:T(8,128)S(1)} custom-call(s32[2]{0:T(128)S(1)} %pad_add_fusion.place_ref, bf16[24,128,128]{2,1,0:T(8,128)(2,1)S(1)} %collective-permute-done.right_ref.right_more_ref, bf16[24,128,128]{2,1,0:T(8,128)(2,1)S(1)} %collective-permute-done.right_ref.right_more_ref, ...), custom_call_target="tpu_custom_call" | custom-call | flops 4000000000 | bytes 4000000 | tf_op jit(solution)/shard_map/border_pairs/pallas_call | solution.py:354
  27.4 1.9 %collective-permute-start.4 = (f32[40,128]{1,0:T(8,128)S(1)}, f32[40,128]{1,0:T(8,128)S(1)}, u32[]{:S(2)}, u32[]{:S(2)}) collective-permute-start(f32[40,128]{1,0:T(8,128)S(1)} %border_pairs.1), channel_id=1, source_target_pairs={{0,3},{1,0},{2,1},{3,2},{4,7},{5,4},{6,5},{7,6},{8,11},{9,8},{10,9... | collective-permute-start | bytes 61448 | tf_op jit(solution)/shard_map/ppermute | solution.py:294
  29.3 0.5 collective-permute-start.3
  29.8 0.6 %collective-permute-start.2 = (f32[40,128]{1,0:T(8,128)S(1)}, f32[40,128]{1,0:T(8,128)S(1)}, u32[]{:S(2)}, u32[]{:S(2)}) collective-permute-start(f32[40,128]{1,0:T(8,128)S(1)} %border_pairs.1), channel_id=1, source_target_pairs={{0,1},{1,2},{2,3},{3,0},{4,5},{5,6},{6,7},{7,4},{8,9},{9,10},{10,1... | collective-permute-start | bytes 61448 | tf_op jit(solution)/shard_map/ppermute | solution.py:294
  30.4 0.0 collective-permute-done.4
  30.4 3.4 %collective-permute-done.3 = f32[40,128]{1,0:T(8,128)S(1)} collective-permute-done((f32[40,128]{1,0:T(8,128)S(1)}, f32[40,128]{1,0:T(8,128)S(1)}, u32[]{:S(2)}, u32[]{:S(2)}) %collective-permute-start.3) | collective-permute-done | bytes 20512 | tf_op jit(solution)/shard_map/ppermute | solution.py:294
  33.8 0.4 collective-permute-done.2
  34.2 0.6 %collective-permute-start.6 = (f32[40,128]{1,0:T(8,128)S(1)}, f32[40,128]{1,0:T(8,128)S(1)}, u32[]{:S(2)}, u32[]{:S(2)}) collective-permute-start(f32[40,128]{1,0:T(8,128)S(1)} %add_add_fusion), channel_id=1, source_target_pairs={{0,252},{4,0},{8,4},{12,8},{16,12},{20,16},{24,20},{28,24},{32,28}... | collective-permute-start | bytes 61448 | tf_op jit(solution)/shard_map/ppermute | solution.py:294
  34.9 1.3 %collective-permute-start.5 = (f32[40,128]{1,0:T(8,128)S(1)}, f32[40,128]{1,0:T(8,128)S(1)}, u32[]{:S(2)}, u32[]{:S(2)}) collective-permute-start(f32[40,128]{1,0:T(8,128)S(1)} %add_add_fusion), channel_id=1, source_target_pairs={{0,4},{4,8},{8,12},{12,16},{16,20},{20,24},{24,28},{28,32},{32,36}... | collective-permute-start | bytes 61448 | tf_op jit(solution)/shard_map/ppermute | solution.py:294
  36.1 1.4 %collective-permute-done.6 = f32[40,128]{1,0:T(8,128)S(1)} collective-permute-done((f32[40,128]{1,0:T(8,128)S(1)}, f32[40,128]{1,0:T(8,128)S(1)}, u32[]{:S(2)}, u32[]{:S(2)}) %collective-permute-start.6) | collective-permute-done | bytes 20512 | tf_op jit(solution)/shard_map/ppermute | solution.py:294
  37.5 3.6 %collective-permute-done.5 = f32[40,128]{1,0:T(8,128)S(1)} collective-permute-done((f32[40,128]{1,0:T(8,128)S(1)}, f32[40,128]{1,0:T(8,128)S(1)}, u32[]{:S(2)}, u32[]{:S(2)}) %collective-permute-start.5) | collective-permute-done | bytes 20512 | tf_op jit(solution)/shard_map/ppermute | solution.py:294
  41.1 5.0 %collective-permute-start.8 = (f32[3,40,128]{2,1,0:T(8,128)S(1)}, f32[3,40,128]{2,1,0:T(8,128)S(1)}, u32[]{:S(2)}, u32[]{:S(2)}) collective-permute-start(f32[3,40,128]{2,1,0:T(8,128)S(1)} %pad_maximum_fusion.near_ref), channel_id=1, source_target_pairs={{0,244},{4,248},{8,252},{12,0},{16,4},{20,8},{24,12},{28,16},{32,2... | collective-permute-start | bytes 184328 | tf_op jit(solution)/shard_map/ppermute | solution.py:294
  46.1 0.0 collective-permute-start.7
  46.1 1.3 %collective-permute-done.8.high_ref = f32[3,40,128]{2,1,0:T(8,128)S(1)} collective-permute-done((f32[3,40,128]{2,1,0:T(8,128)S(1)}, f32[3,40,128]{2,1,0:T(8,128)S(1)}, u32[]{:S(2)}, u32[]{:S(2)}) %collective-permute-start.8) | collective-permute-done | bytes 61472 | tf_op jit(solution)/shard_map/ppermute | solution.py:294
  47.4 6.1 %collective-permute-done.7.low_ref = f32[3,40,128]{2,1,0:T(8,128)S(1)} collective-permute-done((f32[3,40,128]{2,1,0:T(8,128)S(1)}, f32[3,40,128]{2,1,0:T(8,128)S(1)}, u32[]{:S(2)}, u32[]{:S(2)}) %collective-permute-start.7) | collective-permute-done | bytes 61472 | tf_op jit(solution)/shard_map/ppermute | solution.py:294
  53.5 2.1 %relax.1 = (f32[2,6,2,8]{3,2,1,0:T(2,128)}, f32[2,6,3,2,8]{4,3,2,1,0:T(2,128)}) custom-call(s32[2]{0:T(128)S(1)} %pad_add_fusion.place_ref, f32[3,40,128]{2,1,0:T(8,128)S(1)} %pad_maximum_fusion.near_ref, f32[3,40,128]{2,1,0:T(8,128)S(1)} %collective-permute-done.7.low_ref, f32[3,40,128]{2,1,0:T(8,128)S(1)} %collective-permute-done.8.high_ref), custom_call_target="tpu_custom_call" | custom-call | tf_op jit(solution)/shard_map/relax/pallas_call | solution.py:383
  (2 shorter events, 0.0 us)
Async XLA Ops:
  0.6 1.9 %copy-start = (bf16[6,2,8,128,128]{4,3,2,1,0:T(8,128)(2,1)S(1)}, bf16[6,2,8,128,128]{4,3,2,1,0:T(8,128)(2,1)}, u32[]{:S(2)}) copy-start(bf16[6,2,8,128,128]{4,3,2,1,0:T(8,128)(2,1)} %param.4) | copy-start | bytes 9437188
  2.7 18.1 %collective-permute-start = (bf16[24,128,128]{2,1,0:T(8,128)(2,1)S(1)}, bf16[24,128,128]{2,1,0:T(8,128)(2,1)S(1)}, u32[]{:S(2)}, u32[]{:S(2)}) collective-permute-start(bf16[24,128,128]{2,1,0:T(8,128)(2,1)S(1)} %get-tuple-element.6), channel_id=1, source_target_pairs={{4,0},{8,4},{12,8},{16,12},{20,16},{24,20},{28,24},{32,28},{36,32}... | collective-permute-start | bytes 2359304 | tf_op jit(solution)/shard_map/ppermute | solution.py:289
  7.9 13.0 %collective-permute-start.1 = (bf16[24,128,128]{2,1,0:T(8,128)(2,1)S(1)}, bf16[24,128,128]{2,1,0:T(8,128)(2,1)S(1)}, u32[]{:S(2)}, u32[]{:S(2)}) collective-permute-start(bf16[24,128,128]{2,1,0:T(8,128)(2,1)S(1)} %get-tuple-element.7), channel_id=1, source_target_pairs={{0,4},{4,8},{8,12},{12,16},{16,20},{20,24},{24,28},{28,32},{32,36}... | collective-permute-start | bytes 2359304 | tf_op jit(solution)/shard_map/ppermute | solution.py:289
  10.6 1.9 %copy-start.1 = (bf16[6,2,8,128,128]{4,3,2,1,0:T(8,128)(2,1)S(1)}, bf16[6,2,8,128,128]{4,3,2,1,0:T(8,128)(2,1)}, u32[]{:S(2)}) copy-start(bf16[6,2,8,128,128]{4,3,2,1,0:T(8,128)(2,1)} %param.4) | copy-start | bytes 9437188
  12.5 1.0 %copy-start.3 = (bf16[656,256]{1,0:T(8,128)(2,1)S(1)}, bf16[656,256]{1,0:T(8,128)(2,1)}, u32[]{:S(2)}) copy-start(bf16[656,256]{1,0:T(8,128)(2,1)} %constant.11.clone.tabs_ref) | copy-start | bytes 1007620
  13.5 7.3 %copy-start.2 = (f32[2,6,2,8]{3,2,1,0:T(2,128)S(1)}, f32[2,6,2,8]{3,2,1,0:T(2,128)}, u32[]{:S(2)}) copy-start(f32[2,6,2,8]{3,2,1,0:T(2,128)} %nodes_ref.1) | copy-start | bytes 2308
  13.5 7.3 %copy-start.4 = (bf16[656,256]{1,0:T(8,128)(2,1)S(1)}, bf16[656,256]{1,0:T(8,128)(2,1)}, u32[]{:S(2)}) copy-start(bf16[656,256]{1,0:T(8,128)(2,1)} %constant.11.clone.tabs_ref) | copy-start | bytes 1007620
  20.8 1.9 %copy-start.5 = (bf16[16,5,80,256]{3,2,1,0:T(8,128)(2,1)S(1)}, bf16[16,5,80,256]{3,2,1,0:T(8,128)(2,1)}, u32[]{:S(2)}) copy-start(bf16[16,5,80,256]{3,2,1,0:T(8,128)(2,1)} %get-tuple-element.8.kept_ref) | copy-start | bytes 9830404
  27.4 3.1 %collective-permute-start.4 = (f32[40,128]{1,0:T(8,128)S(1)}, f32[40,128]{1,0:T(8,128)S(1)}, u32[]{:S(2)}, u32[]{:S(2)}) collective-permute-start(f32[40,128]{1,0:T(8,128)S(1)} %border_pairs.1), channel_id=1, source_target_pairs={{0,3},{1,0},{2,1},{3,2},{4,7},{5,4},{6,5},{7,6},{8,11},{9,8},{10,9... | collective-permute-start | bytes 61448 | tf_op jit(solution)/shard_map/ppermute | solution.py:294
  29.3 4.5 %collective-permute-start.3 = (f32[40,128]{1,0:T(8,128)S(1)}, f32[40,128]{1,0:T(8,128)S(1)}, u32[]{:S(2)}, u32[]{:S(2)}) collective-permute-start(f32[40,128]{1,0:T(8,128)S(1)} %border_pairs.1), channel_id=1, source_target_pairs={{0,2},{1,3},{2,0},{3,1},{4,6},{5,7},{6,4},{7,5},{8,10},{9,11},{10,... | collective-permute-start | bytes 61448 | tf_op jit(solution)/shard_map/ppermute | solution.py:294
  29.8 4.4 %collective-permute-start.2 = (f32[40,128]{1,0:T(8,128)S(1)}, f32[40,128]{1,0:T(8,128)S(1)}, u32[]{:S(2)}, u32[]{:S(2)}) collective-permute-start(f32[40,128]{1,0:T(8,128)S(1)} %border_pairs.1), channel_id=1, source_target_pairs={{0,1},{1,2},{2,3},{3,0},{4,5},{5,6},{6,7},{7,4},{8,9},{9,10},{10,1... | collective-permute-start | bytes 61448 | tf_op jit(solution)/shard_map/ppermute | solution.py:294
  34.2 3.3 %collective-permute-start.6 = (f32[40,128]{1,0:T(8,128)S(1)}, f32[40,128]{1,0:T(8,128)S(1)}, u32[]{:S(2)}, u32[]{:S(2)}) collective-permute-start(f32[40,128]{1,0:T(8,128)S(1)} %add_add_fusion), channel_id=1, source_target_pairs={{0,252},{4,0},{8,4},{12,8},{16,12},{20,16},{24,20},{28,24},{32,28}... | collective-permute-start | bytes 61448 | tf_op jit(solution)/shard_map/ppermute | solution.py:294
  34.9 6.2 %collective-permute-start.5 = (f32[40,128]{1,0:T(8,128)S(1)}, f32[40,128]{1,0:T(8,128)S(1)}, u32[]{:S(2)}, u32[]{:S(2)}) collective-permute-start(f32[40,128]{1,0:T(8,128)S(1)} %add_add_fusion), channel_id=1, source_target_pairs={{0,4},{4,8},{8,12},{12,16},{16,20},{20,24},{24,28},{28,32},{32,36}... | collective-permute-start | bytes 61448 | tf_op jit(solution)/shard_map/ppermute | solution.py:294
  41.1 6.3 %collective-permute-start.8 = (f32[3,40,128]{2,1,0:T(8,128)S(1)}, f32[3,40,128]{2,1,0:T(8,128)S(1)}, u32[]{:S(2)}, u32[]{:S(2)}) collective-permute-start(f32[3,40,128]{2,1,0:T(8,128)S(1)} %pad_maximum_fusion.near_ref), channel_id=1, source_target_pairs={{0,244},{4,248},{8,252},{12,0},{16,4},{20,8},{24,12},{28,16},{32,2... | collective-permute-start | bytes 184328 | tf_op jit(solution)/shard_map/ppermute | solution.py:294
  46.1 7.4 %collective-permute-start.7 = (f32[3,40,128]{2,1,0:T(8,128)S(1)}, f32[3,40,128]{2,1,0:T(8,128)S(1)}, u32[]{:S(2)}, u32[]{:S(2)}) collective-permute-start(f32[3,40,128]{2,1,0:T(8,128)S(1)} %pad_maximum_fusion.near_ref), channel_id=1, source_target_pairs={{0,12},{4,16},{8,20},{12,24},{16,28},{20,32},{24,36},{28,40},{32,4... | collective-permute-start | bytes 184328 | tf_op jit(solution)/shard_map/ppermute | solution.py:294

commit v4 on v3

--- a/solution.py
+++ b/solution.py
@@ -15,11 +15,8 @@
 LENGTH = 128
 HALF = 64
 LANES = 128
-PACKS = 3
-PACK_VMEM = 8
-PACK_OUT = pl.BlockSpec(memory_space=pl.ANY)
-OWN_VMEM = 48
-BORDER_VMEM = 48
+OWN_VMEM = 32
+BORDER_VMEM = 32
 KEPT = 5
 FULL = 80
 
@@ -137,19 +134,15 @@
     return acc
 
 
-def pack_kernel(patches_ref, first_ref, last_ref, sems):
+def pack_kernel(patches_ref, first_ref, last_ref, all_ref, sems):
     count = first_ref.shape[0]
     begin = patches_ref.shape[0] - count
-    each = count // PACKS
-    copies = []
-    for n in range(2 * PACKS):
-        out_ref, at = (first_ref, n * each) if n < PACKS else (last_ref, (n - PACKS) * each)
-        source = at if n < PACKS else begin + at
-        copies.append(
-            pltpu.make_async_copy(
-                patches_ref.at[pl.ds(source, each)], out_ref.at[pl.ds(at, each)], sems.at[n]
-            )
-        )
+    moves = [
+        (patches_ref.at[pl.ds(0, count)], first_ref),
+        (patches_ref.at[pl.ds(begin, count)], last_ref),
+        (patches_ref, all_ref),
+    ]
+    copies = [pltpu.make_async_copy(*move, sems.at[n]) for n, move in enumerate(moves)]
     for copy in copies:
         copy.start()
     for copy in copies:
@@ -217,11 +210,16 @@
             [nodes_ref[0, :, 0], nodes_ref[0, :, 1], gap, nodes_ref[1, :, 0], nodes_ref[1, :, 1], gap],
             axis=1,
         )
-        flags = jnp.concatenate(
-            [flags_ref[...].astype(jnp.float32), jnp.zeros((6, LANES - 3), jnp.float32)], axis=1
-        )
-        ahead = place_ref[1] * 6 + lax.broadcasted_iota(jnp.int32, (6, LANES), 0)
-        ahead = ahead + 1 + lax.broadcasted_iota(jnp.int32, (6, LANES), 1)
+        given = flags_ref[...].astype(jnp.float32)
+        section = lax.broadcasted_iota(jnp.int32, (6, 6), 0)
+        diagonal = section == lax.broadcasted_iota(jnp.int32, (6, 6), 1)
+        place = lax.broadcasted_iota(jnp.int32, (6, LANES), 1)
+        flags = jnp.zeros((6, LANES), jnp.float32)
+        for o in (1, 2, 3):
+            wide = jnp.broadcast_to(given[o - 1 : o], (6, 6))
+            column = jnp.sum(jnp.where(diagonal, wide, 0.0), axis=1, keepdims=True)
+            flags = jnp.where(place == o - 1, column, flags)
+        ahead = place_ref[1] * 6 + lax.broadcasted_iota(jnp.int32, (6, LANES), 0) + 1 + place
         flags = jnp.where(ahead < sections, flags, 0.0)
         two = jnp.zeros((2, LANES), jnp.float32)
         message = jnp.concatenate([u, two, flags, two, acc_ref[...]], axis=0)
@@ -315,16 +313,18 @@
         return pl.BlockSpec((step, LENGTH, LENGTH), at)
 
     flat = patches.reshape(local * count, LENGTH, LENGTH)
-    first, last = pl.pallas_call(
+    first, last, held = pl.pallas_call(
         pack_kernel,
-        in_specs=[pl.BlockSpec(memory_space=pltpu.HBM)],
-        out_specs=[PACK_OUT] * 2,
-        out_shape=[jax.ShapeDtypeStruct((sent, LENGTH, LENGTH), patches.dtype)] * 2,
-        scratch_shapes=[
-            pltpu.SemaphoreType.DMA((2 * PACKS,)),
-        ],
-        compiler_params=pltpu.CompilerParams(vmem_limit_bytes=PACK_VMEM * 1024 * 1024),
-        cost_estimate=pl.CostEstimate(flops=0, bytes_accessed=3_000_000, transcendentals=0),
+        in_specs=[anywhere],
+        out_specs=[anywhere] * 3,
+        out_shape=[
+            jax.ShapeDtypeStruct((sent, LENGTH, LENGTH), patches.dtype),
+            jax.ShapeDtypeStruct((sent, LENGTH, LENGTH), patches.dtype),
+            jax.ShapeDtypeStruct(flat.shape, patches.dtype),
+        ],
+        scratch_shapes=[pltpu.SemaphoreType.DMA((4,))],
+        compiler_params=pltpu.CompilerParams(vmem_limit_bytes=8 * 1024 * 1024),
+        cost_estimate=pl.CostEstimate(flops=0, bytes_accessed=6_000_000, transcendentals=0),
         name="pack",
     )(flat)
     from_right = shifted(first, "sec", -1)
@@ -348,7 +348,7 @@
         compiler_params=own_params,
         cost_estimate=pl.CostEstimate(flops=8_000_000_000, bytes_accessed=6_000_000, transcendentals=0),
         name="own_pairs",
-    )(patches.reshape(local, count, LENGTH, LENGTH), tabs)
+    )(held.reshape(local, count, LENGTH, LENGTH), tabs)
 
     place = jnp.stack([lax.axis_index("tile"), lax.axis_index("sec")]).astype(jnp.int32)
     message = pl.pallas_call(
@@ -363,7 +363,7 @@
             pl.BlockSpec((step, KEPT, FULL, 2 * LANES), lambda n: (n, 0, 0, 0)),
             whole(*tabs.shape),
             whole(24, LANES),
-            whole(*pair_flags.shape),
+            whole(reach, local),
             whole(*nodes.shape),
         ],
         out_specs=whole(40, LANES),
@@ -372,7 +372,7 @@
         compiler_params=border_params,
         cost_estimate=pl.CostEstimate(flops=4_000_000_000, bytes_accessed=4_000_000, transcendentals=0),
         name="border_pairs",
-    )(place, from_right, from_right, from_left, from_left, kept, tabs, own, pair_flags, nodes)
+    )(place, from_right, from_right, from_left, from_left, kept, tabs, own, pair_flags.T, nodes)
 
     joined = message
     for by in range(1, lax.axis_size("tile")):

time: 55.9 us -> 57.3 us (1.025)
  the two profiles are of different devices: /device:TPU:1 before, /device:TPU:113 now
where the time goes in v4:
time: 57.3 us; the launch traced here: 57.1 us
  starting transfers between devices  24.9 us (43%)
  Pallas kernels  15.1 us (26%)
  waiting for transfers between devices  14.5 us (25%)
  local copies, waits for them, and re-layouts  1.89 us (3%)
  between operations  0.68 us (1%)
    ppermute x7, starting transfers between devices, turned_by(): lax.ppermute(value, axis, [(i, (i + by) % count) for i in range(count)])  19.3 us
    ppermute x7, waiting for transfers between devices, turned_by(): lax.ppermute(value, axis, [(i, (i + by) % count) for i in range(count)])  11.9 us
    pallas_call x1, Pallas kernels, shards(): pl.pallas_call(own_kernel, grid=(count // step,), in_specs=[pl.BlockSpec(...  6.59 us
    ppermute x2, starting transfers between devices, shifted(): return lax.ppermute(value, axis, pairs)  5.56 us
    pallas_call x1, Pallas kernels, shards(): pl.pallas_call(functools.partial(next_kernel, sections=sections), grid=(c...  5.24 us
    ppermute x2, waiting for transfers between devices, shifted(): return lax.ppermute(value, axis, pairs)  2.55 us
    pallas_call x1, Pallas kernels, shards(): pl.pallas_call(relax_kernel, in_specs=[smem] + [vmem] * 3, out_specs=[vme...  2.05 us
    unnamed x8, local copies, waits for them, and re-layouts  1.89 us
  transfers between devices with their start and end apart: 9, of which 8 were waited for; matrix products, arithmetic and copies ran while one was open for 0% of the time, Pallas kernels for 12%

profile of v4, /device:TPU:113, one launch (start us, length us, event | category | flops | bytes accessed | tf_op | source)
XLA Modules:
  0.0 57.1 jit_solution(13057607258436253569)
XLA Ops:
  0.6 0.0 copy-start
  0.6 1.9 %copy-done = bf16[6,2,8,128,128]{4,3,2,1,0:T(8,128)(2,1)S(1)} copy-done((bf16[6,2,8,128,128]{4,3,2,1,0:T(8,128)(2,1)S(1)}, bf16[6,2,8,128,128]{4,3,2,1,0:T(8,128)(2,1)}, u32[]{:S(2)}) %copy-start) | copy-done | bytes 3145752
  2.5 0.0 copy-start.3
  2.5 1.2 %pack.1 = (bf16[24,128,128]{2,1,0:T(8,128)(2,1)}, bf16[24,128,128]{2,1,0:T(8,128)(2,1)}, bf16[96,128,128]{2,1,0:T(8,128)(2,1)S(1)}) custom-call(bf16[96,128,128]{2,1,0:T(8,128)(2,1)S(1)} %bitcast.8), custom_call_target="tpu_custom_call" | custom-call | bytes 6000000 | tf_op jit(solution)/shard_map/pack/pallas_call | solution.py:316
  3.7 2.6 %collective-permute-start = (bf16[24,128,128]{2,1,0:T(8,128)(2,1)}, bf16[24,128,128]{2,1,0:T(8,128)(2,1)}, u32[]{:S(2)}, u32[]{:S(2)}) collective-permute-start(bf16[24,128,128]{2,1,0:T(8,128)(2,1)} %get-tuple-element.7), channel_id=1, source_target_pairs={{4,0},{8,4},{12,8},{16,12},{20,16},{24,20},{28,24},{32,28},{36,32}... | collective-permute-start | bytes 2359304 | tf_op jit(solution)/shard_map/ppermute | solution.py:287
  6.3 3.0 %collective-permute-start.1 = (bf16[24,128,128]{2,1,0:T(8,128)(2,1)}, bf16[24,128,128]{2,1,0:T(8,128)(2,1)}, u32[]{:S(2)}, u32[]{:S(2)}) collective-permute-start(bf16[24,128,128]{2,1,0:T(8,128)(2,1)} %get-tuple-element.8), channel_id=1, source_target_pairs={{0,4},{4,8},{8,12},{12,16},{16,20},{20,24},{24,28},{28,32},{32,36}... | collective-permute-start | bytes 2359304 | tf_op jit(solution)/shard_map/ppermute | solution.py:287
  9.3 0.1 pad_add_fusion.place_ref
  9.4 0.0 copy-done.3
  9.4 0.0 copy-start.1
  9.4 0.0 copy-start.2
  9.4 6.6 %own_pairs.1 = (f32[24,128]{1,0:T(8,128)S(1)}, bf16[16,5,80,256]{3,2,1,0:T(8,128)(2,1)S(1)}) custom-call(bf16[6,16,128,128]{3,2,1,0:T(8,128)(2,1)S(1)} %bitcast.9, bf16[656,256]{1,0:T(8,128)(2,1)S(1)} %copy-done.3), custom_call_target="tpu_custom_call" | custom-call | flops 8000000000 | bytes 6000000 | tf_op jit(solution)/shard_map/own_pairs/pallas_call | solution.py:333
  16.0 1.7 %collective-permute-done.right_ref.right_more_ref = bf16[24,128,128]{2,1,0:T(8,128)(2,1)} collective-permute-done((bf16[24,128,128]{2,1,0:T(8,128)(2,1)}, bf16[24,128,128]{2,1,0:T(8,128)(2,1)}, u32[]{:S(2)}, u32[]{:S(2)}) %collective-permute-start) | collective-permute-done | bytes 786464 | tf_op jit(solution)/shard_map/ppermute | solution.py:287
  17.7 0.9 %collective-permute-done.1.left_ref.left_more_ref = bf16[24,128,128]{2,1,0:T(8,128)(2,1)} collective-permute-done((bf16[24,128,128]{2,1,0:T(8,128)(2,1)}, bf16[24,128,128]{2,1,0:T(8,128)(2,1)}, u32[]{:S(2)}, u32[]{:S(2)}) %collective-permute-start.1) | collective-permute-done | bytes 786464 | tf_op jit(solution)/shard_map/ppermute | solution.py:287
  18.5 0.0 copy-done.1
  18.5 0.0 copy-done.2
  18.5 5.2 %border_pairs.1 = f32[40,128]{1,0:T(8,128)S(1)} custom-call(s32[2]{0:T(128)S(1)} %pad_add_fusion.place_ref, bf16[24,128,128]{2,1,0:T(8,128)(2,1)} %collective-permute-done.right_ref.right_more_ref, bf16[24,128,128]{2,1,0:T(8,128)(2,1)} %collective-permute-done.right_ref.right_more_ref, bf16[24,128,128]{2,1,0:T(8,128)(2,1)} %collective-permute-done.1.left_ref.left_more_ref, ...), custom_call_target="tpu_custom_call" | custom-call | flops 4000000000 | bytes 4000000 | tf_op jit(solution)/shard_map/border_pairs/pallas_call | solution.py:354
  23.8 1.3 %collective-permute-start.2 = (f32[40,128]{1,0:T(8,128)S(1)}, f32[40,128]{1,0:T(8,128)S(1)}, u32[]{:S(2)}, u32[]{:S(2)}) collective-permute-start(f32[40,128]{1,0:T(8,128)S(1)} %border_pairs.1), channel_id=1, source_target_pairs={{0,1},{1,2},{2,3},{3,0},{4,5},{5,6},{6,7},{7,4},{8,9},{9,10},{10,1... | collective-permute-start | bytes 61448 | tf_op jit(solution)/shard_map/ppermute | solution.py:292
  25.1 2.4 %collective-permute-start.3 = (f32[40,128]{1,0:T(8,128)S(1)}, f32[40,128]{1,0:T(8,128)S(1)}, u32[]{:S(2)}, u32[]{:S(2)}) collective-permute-start(f32[40,128]{1,0:T(8,128)S(1)} %border_pairs.1), channel_id=1, source_target_pairs={{0,2},{1,3},{2,0},{3,1},{4,6},{5,7},{6,4},{7,5},{8,10},{9,11},{10,... | collective-permute-start | bytes 61448 | tf_op jit(solution)/shard_map/ppermute | solution.py:292
  27.5 1.2 %collective-permute-start.4 = (f32[40,128]{1,0:T(8,128)S(1)}, f32[40,128]{1,0:T(8,128)S(1)}, u32[]{:S(2)}, u32[]{:S(2)}) collective-permute-start(f32[40,128]{1,0:T(8,128)S(1)} %border_pairs.1), channel_id=1, source_target_pairs={{0,3},{1,0},{2,1},{3,2},{4,7},{5,4},{6,5},{7,6},{8,11},{9,8},{10,9... | collective-permute-start | bytes 61448 | tf_op jit(solution)/shard_map/ppermute | solution.py:292
  28.7 0.0 collective-permute-done.2
  28.7 0.5 collective-permute-done.3
  29.2 0.9 %collective-permute-done.4 = f32[40,128]{1,0:T(8,128)S(1)} collective-permute-done((f32[40,128]{1,0:T(8,128)S(1)}, f32[40,128]{1,0:T(8,128)S(1)}, u32[]{:S(2)}, u32[]{:S(2)}) %collective-permute-start.4) | collective-permute-done | bytes 20512 | tf_op jit(solution)/shard_map/ppermute | solution.py:292
  30.2 4.3 %collective-permute-start.5 = (f32[40,128]{1,0:T(8,128)S(1)}, f32[40,128]{1,0:T(8,128)S(1)}, u32[]{:S(2)}, u32[]{:S(2)}) collective-permute-start(f32[40,128]{1,0:T(8,128)S(1)} %add_add_fusion), channel_id=1, source_target_pairs={{0,4},{4,8},{8,12},{12,16},{16,20},{20,24},{24,28},{28,32},{32,36}... | collective-permute-start | bytes 61448 | tf_op jit(solution)/shard_map/ppermute | solution.py:292
  34.4 0.0 collective-permute-start.6
  34.4 0.9 %collective-permute-done.5 = f32[40,128]{1,0:T(8,128)S(1)} collective-permute-done((f32[40,128]{1,0:T(8,128)S(1)}, f32[40,128]{1,0:T(8,128)S(1)}, u32[]{:S(2)}, u32[]{:S(2)}) %collective-permute-start.5) | collective-permute-done | bytes 20512 | tf_op jit(solution)/shard_map/ppermute | solution.py:292
  35.3 2.3 %collective-permute-done.6 = f32[40,128]{1,0:T(8,128)S(1)} collective-permute-done((f32[40,128]{1,0:T(8,128)S(1)}, f32[40,128]{1,0:T(8,128)S(1)}, u32[]{:S(2)}, u32[]{:S(2)}) %collective-permute-start.6) | collective-permute-done | bytes 20512 | tf_op jit(solution)/shard_map/ppermute | solution.py:292
  37.6 10.2 %collective-permute-start.7 = (f32[3,40,128]{2,1,0:T(8,128)S(1)}, f32[3,40,128]{2,1,0:T(8,128)S(1)}, u32[]{:S(2)}, u32[]{:S(2)}) collective-permute-start(f32[3,40,128]{2,1,0:T(8,128)S(1)} %pad_maximum_fusion.near_ref), channel_id=1, source_target_pairs={{0,12},{4,16},{8,20},{12,24},{16,28},{20,32},{24,36},{28,40},{32,4... | collective-permute-start | bytes 184328 | tf_op jit(solution)/shard_map/ppermute | solution.py:292
  47.8 0.0 collective-permute-start.8
  47.8 1.3 %collective-permute-done.7.low_ref = f32[3,40,128]{2,1,0:T(8,128)S(1)} collective-permute-done((f32[3,40,128]{2,1,0:T(8,128)S(1)}, f32[3,40,128]{2,1,0:T(8,128)S(1)}, u32[]{:S(2)}, u32[]{:S(2)}) %collective-permute-start.7) | collective-permute-done | bytes 61472 | tf_op jit(solution)/shard_map/ppermute | solution.py:292
  49.1 6.0 %collective-permute-done.8.high_ref = f32[3,40,128]{2,1,0:T(8,128)S(1)} collective-permute-done((f32[3,40,128]{2,1,0:T(8,128)S(1)}, f32[3,40,128]{2,1,0:T(8,128)S(1)}, u32[]{:S(2)}, u32[]{:S(2)}) %collective-permute-start.8) | collective-permute-done | bytes 61472 | tf_op jit(solution)/shard_map/ppermute | solution.py:292
  55.1 2.1 %relax.1 = (f32[2,6,2,8]{3,2,1,0:T(2,128)}, f32[2,6,3,2,8]{4,3,2,1,0:T(2,128)}) custom-call(s32[2]{0:T(128)S(1)} %pad_add_fusion.place_ref, f32[3,40,128]{2,1,0:T(8,128)S(1)} %pad_maximum_fusion.near_ref, f32[3,40,128]{2,1,0:T(8,128)S(1)} %collective-permute-done.7.low_ref, f32[3,40,128]{2,1,0:T(8,128)S(1)} %collective-permute-done.8.high_ref), custom_call_target="tpu_custom_call" | custom-call | tf_op jit(solution)/shard_map/relax/pallas_call | solution.py:383
  (2 shorter events, 0.0 us)
Async XLA Ops:
  0.6 1.9 %copy-start = (bf16[6,2,8,128,128]{4,3,2,1,0:T(8,128)(2,1)S(1)}, bf16[6,2,8,128,128]{4,3,2,1,0:T(8,128)(2,1)}, u32[]{:S(2)}) copy-start(bf16[6,2,8,128,128]{4,3,2,1,0:T(8,128)(2,1)} %param.4) | copy-start | bytes 9437188
  2.5 6.9 %copy-start.3 = (bf16[656,256]{1,0:T(8,128)(2,1)S(1)}, bf16[656,256]{1,0:T(8,128)(2,1)}, u32[]{:S(2)}) copy-start(bf16[656,256]{1,0:T(8,128)(2,1)} %constant.11.clone.tabs_ref) | copy-start | bytes 1007620
  3.7 13.9 %collective-permute-start = (bf16[24,128,128]{2,1,0:T(8,128)(2,1)}, bf16[24,128,128]{2,1,0:T(8,128)(2,1)}, u32[]{:S(2)}, u32[]{:S(2)}) collective-permute-start(bf16[24,128,128]{2,1,0:T(8,128)(2,1)} %get-tuple-element.7), channel_id=1, source_target_pairs={{4,0},{8,4},{12,8},{16,12},{20,16},{24,20},{28,24},{32,28},{36,32}... | collective-permute-start | bytes 2359304 | tf_op jit(solution)/shard_map/ppermute | solution.py:287
  6.3 12.2 %collective-permute-start.1 = (bf16[24,128,128]{2,1,0:T(8,128)(2,1)}, bf16[24,128,128]{2,1,0:T(8,128)(2,1)}, u32[]{:S(2)}, u32[]{:S(2)}) collective-permute-start(bf16[24,128,128]{2,1,0:T(8,128)(2,1)} %get-tuple-element.8), channel_id=1, source_target_pairs={{0,4},{4,8},{8,12},{12,16},{16,20},{20,24},{24,28},{28,32},{32,36}... | collective-permute-start | bytes 2359304 | tf_op jit(solution)/shard_map/ppermute | solution.py:287
  9.4 9.1 %copy-start.1 = (f32[2,6,2,8]{3,2,1,0:T(2,128)S(1)}, f32[2,6,2,8]{3,2,1,0:T(2,128)}, u32[]{:S(2)}) copy-start(f32[2,6,2,8]{3,2,1,0:T(2,128)} %nodes_ref.1) | copy-start | bytes 2308
  9.4 9.1 %copy-start.2 = (s32[6,3]{0,1:T(4,128)S(1)}, s32[6,3]{0,1:T(4,128)}, u32[]{:S(2)}) copy-start(s32[6,3]{0,1:T(4,128)} %param.5) | copy-start | bytes 220
  23.8 4.9 %collective-permute-start.2 = (f32[40,128]{1,0:T(8,128)S(1)}, f32[40,128]{1,0:T(8,128)S(1)}, u32[]{:S(2)}, u32[]{:S(2)}) collective-permute-start(f32[40,128]{1,0:T(8,128)S(1)} %border_pairs.1), channel_id=1, source_target_pairs={{0,1},{1,2},{2,3},{3,0},{4,5},{5,6},{6,7},{7,4},{8,9},{9,10},{10,1... | collective-permute-start | bytes 61448 | tf_op jit(solution)/shard_map/ppermute | solution.py:292
  25.1 4.1 %collective-permute-start.3 = (f32[40,128]{1,0:T(8,128)S(1)}, f32[40,128]{1,0:T(8,128)S(1)}, u32[]{:S(2)}, u32[]{:S(2)}) collective-permute-start(f32[40,128]{1,0:T(8,128)S(1)} %border_pairs.1), channel_id=1, source_target_pairs={{0,2},{1,3},{2,0},{3,1},{4,6},{5,7},{6,4},{7,5},{8,10},{9,11},{10,... | collective-permute-start | bytes 61448 | tf_op jit(solution)/shard_map/ppermute | solution.py:292
  27.5 2.6 %collective-permute-start.4 = (f32[40,128]{1,0:T(8,128)S(1)}, f32[40,128]{1,0:T(8,128)S(1)}, u32[]{:S(2)}, u32[]{:S(2)}) collective-permute-start(f32[40,128]{1,0:T(8,128)S(1)} %border_pairs.1), channel_id=1, source_target_pairs={{0,3},{1,0},{2,1},{3,2},{4,7},{5,4},{6,5},{7,6},{8,11},{9,8},{10,9... | collective-permute-start | bytes 61448 | tf_op jit(solution)/shard_map/ppermute | solution.py:292
  30.2 5.2 %collective-permute-start.5 = (f32[40,128]{1,0:T(8,128)S(1)}, f32[40,128]{1,0:T(8,128)S(1)}, u32[]{:S(2)}, u32[]{:S(2)}) collective-permute-start(f32[40,128]{1,0:T(8,128)S(1)} %add_add_fusion), channel_id=1, source_target_pairs={{0,4},{4,8},{8,12},{12,16},{16,20},{20,24},{24,28},{28,32},{32,36}... | collective-permute-start | bytes 61448 | tf_op jit(solution)/shard_map/ppermute | solution.py:292
  34.4 3.2 %collective-permute-start.6 = (f32[40,128]{1,0:T(8,128)S(1)}, f32[40,128]{1,0:T(8,128)S(1)}, u32[]{:S(2)}, u32[]{:S(2)}) collective-permute-start(f32[40,128]{1,0:T(8,128)S(1)} %add_add_fusion), channel_id=1, source_target_pairs={{0,252},{4,0},{8,4},{12,8},{16,12},{20,16},{24,20},{28,24},{32,28}... | collective-permute-start | bytes 61448 | tf_op jit(solution)/shard_map/ppermute | solution.py:292
  37.6 11.5 %collective-permute-start.7 = (f32[3,40,128]{2,1,0:T(8,128)S(1)}, f32[3,40,128]{2,1,0:T(8,128)S(1)}, u32[]{:S(2)}, u32[]{:S(2)}) collective-permute-start(f32[3,40,128]{2,1,0:T(8,128)S(1)} %pad_maximum_fusion.near_ref), channel_id=1, source_target_pairs={{0,12},{4,16},{8,20},{12,24},{16,28},{20,32},{24,36},{28,40},{32,4... | collective-permute-start | bytes 184328 | tf_op jit(solution)/shard_map/ppermute | solution.py:292
  47.8 7.3 %collective-permute-start.8 = (f32[3,40,128]{2,1,0:T(8,128)S(1)}, f32[3,40,128]{2,1,0:T(8,128)S(1)}, u32[]{:S(2)}, u32[]{:S(2)}) collective-permute-start(f32[3,40,128]{2,1,0:T(8,128)S(1)} %pad_maximum_fusion.near_ref), channel_id=1, source_target_pairs={{0,244},{4,248},{8,252},{12,0},{16,4},{20,8},{24,12},{28,16},{32,2... | collective-permute-start | bytes 184328 | tf_op jit(solution)/shard_map/ppermute | solution.py:292

commit v5 on v4

--- a/solution.py
+++ b/solution.py
@@ -134,12 +134,13 @@
     return acc
 
 
-def pack_kernel(patches_ref, first_ref, last_ref, all_ref, sems):
-    count = first_ref.shape[0]
-    begin = patches_ref.shape[0] - count
+def pack_kernel(place_ref, patches_ref, outer_ref, inner_ref, all_ref, sems):
+    count = outer_ref.shape[0]
+    end = patches_ref.shape[0] - count
+    odd = lax.rem(place_ref[1], 2)
     moves = [
-        (patches_ref.at[pl.ds(0, count)], first_ref),
-        (patches_ref.at[pl.ds(begin, count)], last_ref),
+        (patches_ref.at[pl.ds(odd * end, count)], outer_ref),
+        (patches_ref.at[pl.ds((1 - odd) * end, count)], inner_ref),
         (patches_ref, all_ref),
     ]
     copies = [pltpu.make_async_copy(*move, sems.at[n]) for n, move in enumerate(moves)]
@@ -171,11 +172,12 @@
 
 
 def next_kernel(
-    place_ref, right_ref, right_more_ref, left_ref, left_more_ref, kept_ref, tabs_ref,
+    place_ref, outer_ref, inner_ref, kept_ref, tabs_ref,
     own_ref, flags_ref, nodes_ref, message_ref, acc_ref, *, sections,
 ):
     step = pl.program_id(0)
-    nodes = right_ref.shape[0]
+    nodes = kept_ref.shape[0]
+    odd = lax.rem(place_ref[1], 2) == 1
 
     @pl.when(step == 0)
     def _():
@@ -184,10 +186,15 @@
     early = step == 0
     sign = jnp.where(early, -1.0, 1.0).astype(jnp.float32)
     mate = jnp.where(early, 3, 0)
+    use_outer = early == odd
     inputs = []
     for k in range(nodes):
-        third = jnp.where(early, right_more_ref[k], left_more_ref[k])
-        inputs += [right_ref[k], left_ref[k], third]
+        at = step * nodes + k
+        right = jnp.where(odd, outer_ref[at], inner_ref[at])
+        left = jnp.where(odd, inner_ref[at + nodes], outer_ref[at + nodes])
+        more = jnp.where(early, 2 * nodes, 0) + k
+        third = jnp.where(use_outer, outer_ref[more], inner_ref[more])
+        inputs += [right, left, third]
     spec = spectra(inputs, tabs_ref)
     pairs = []
     for k in range(nodes):
@@ -281,9 +288,11 @@
                 m_out[c, :, o, i, :] = measured[:6, lanes]
 
 
-def shifted(value, axis, by):
+def swapped(value, axis, start):
     count = lax.axis_size(axis)
-    pairs = [(i, i + by) for i in range(count) if 0 <= i + by < count]
+    pairs = []
+    for i in range(start, count - 1, 2):
+        pairs += [(i, i + 1), (i + 1, i)]
     return lax.ppermute(value, axis, pairs)
 
 
@@ -309,26 +318,24 @@
     def whole(*shape):
         return pl.BlockSpec(shape, lambda n: (0,) * len(shape))
 
-    def block(at):
-        return pl.BlockSpec((step, LENGTH, LENGTH), at)
-
     flat = patches.reshape(local * count, LENGTH, LENGTH)
-    first, last, held = pl.pallas_call(
+    place = jnp.stack([lax.axis_index("tile"), lax.axis_index("sec")]).astype(jnp.int32)
+    outer, inner, held = pl.pallas_call(
         pack_kernel,
-        in_specs=[anywhere],
+        in_specs=[smem, anywhere],
         out_specs=[anywhere] * 3,
         out_shape=[
             jax.ShapeDtypeStruct((sent, LENGTH, LENGTH), patches.dtype),
             jax.ShapeDtypeStruct((sent, LENGTH, LENGTH), patches.dtype),
             jax.ShapeDtypeStruct(flat.shape, patches.dtype),
         ],
-        scratch_shapes=[pltpu.SemaphoreType.DMA((4,))],
+        scratch_shapes=[pltpu.SemaphoreType.DMA((3,))],
         compiler_params=pltpu.CompilerParams(vmem_limit_bytes=8 * 1024 * 1024),
         cost_estimate=pl.CostEstimate(flops=0, bytes_accessed=6_000_000, transcendentals=0),
         name="pack",
-    )(flat)
-    from_right = shifted(first, "sec", -1)
-    from_left = shifted(last, "sec", 1)
+    )(place, flat)
+    outer = swapped(outer, "sec", 1)
+    inner = swapped(inner, "sec", 0)
 
     own, kept = pl.pallas_call(
         own_kernel,
@@ -350,16 +357,13 @@
         name="own_pairs",
     )(held.reshape(local, count, LENGTH, LENGTH), tabs)
 
-    place = jnp.stack([lax.axis_index("tile"), lax.axis_index("sec")]).astype(jnp.int32)
     message = pl.pallas_call(
         functools.partial(next_kernel, sections=sections),
         grid=(count // step,),
         in_specs=[
             smem,
-            block(lambda n: (n, 0, 0)),
-            block(lambda n: (2, 0, 0)),
-            block(lambda n: (n + 1, 0, 0)),
-            block(lambda n: (0, 0, 0)),
+            vmem,
+            vmem,
             pl.BlockSpec((step, KEPT, FULL, 2 * LANES), lambda n: (n, 0, 0, 0)),
             whole(*tabs.shape),
             whole(24, LANES),
@@ -372,7 +376,7 @@
         compiler_params=border_params,
         cost_estimate=pl.CostEstimate(flops=4_000_000_000, bytes_accessed=4_000_000, transcendentals=0),
         name="border_pairs",
-    )(place, from_right, from_right, from_left, from_left, kept, tabs, own, pair_flags.T, nodes)
+    )(place, outer, inner, kept, tabs, own, pair_flags.T, nodes)
 
     joined = message
     for by in range(1, lax.axis_size("tile")):

time: 57.3 us -> 52 us (0.908)
  the two profiles are of different devices: /device:TPU:113 before, /device:TPU:1 now
where the time goes in v5:
time: 52 us; the launch traced here: 51.9 us
  starting transfers between devices  20.1 us (39%)
  waiting for transfers between devices  14.8 us (28%)
  Pallas kernels  14.2 us (27%)
  local copies, waits for them, and re-layouts  1.91 us (4%)
  between operations  0.71 us (1%)
    ppermute x7, starting transfers between devices, turned_by(): lax.ppermute(value, axis, [(i, (i + by) % count) for i in range(count)])  15.5 us
    ppermute x7, waiting for transfers between devices, turned_by(): lax.ppermute(value, axis, [(i, (i + by) % count) for i in range(count)])  12 us
    pallas_call x1, Pallas kernels, shards(): pl.pallas_call(own_kernel, grid=(count // step,), in_specs=[pl.BlockSpec(...  6.72 us
    ppermute x2, starting transfers between devices, swapped(): return lax.ppermute(value, axis, pairs)  4.69 us
    pallas_call x1, Pallas kernels, shards(): pl.pallas_call(functools.partial(next_kernel, sections=sections), grid=(c...  4.54 us
    ppermute x2, waiting for transfers between devices, swapped(): return lax.ppermute(value, axis, pairs)  2.81 us
    pallas_call x1, Pallas kernels, shards(): pl.pallas_call(relax_kernel, in_specs=[smem] + [vmem] * 3, out_specs=[vme...  2.05 us
    unnamed x8, local copies, waits for them, and re-layouts  1.91 us
  transfers between devices with their start and end apart: 9, of which 7 were waited for; matrix products, arithmetic and copies ran while one was open for 0% of the time, Pallas kernels for 13%

profile of v5, /device:TPU:1, one launch (start us, length us, event | category | flops | bytes accessed | tf_op | source)
XLA Modules:
  0.0 51.9 jit_solution(16775136107821929010)
XLA Ops:
  0.6 0.1 pad_add_fusion.place_ref
  0.7 0.0 copy-start
  0.7 1.9 %copy-done = bf16[6,2,8,128,128]{4,3,2,1,0:T(8,128)(2,1)S(1)} copy-done((bf16[6,2,8,128,128]{4,3,2,1,0:T(8,128)(2,1)S(1)}, bf16[6,2,8,128,128]{4,3,2,1,0:T(8,128)(2,1)}, u32[]{:S(2)}) %copy-start) | copy-done | bytes 3145752
  2.6 0.0 copy-start.3
  2.6 0.9 %pack.1 = (bf16[24,128,128]{2,1,0:T(8,128)(2,1)S(1)}, bf16[24,128,128]{2,1,0:T(8,128)(2,1)S(1)}, bf16[96,128,128]{2,1,0:T(8,128)(2,1)S(1)}) custom-call(s32[2]{0:T(128)S(1)} %pad_add_fusion.place_ref, bf16[96,128,128]{2,1,0:T(8,128)(2,1)S(1)} %bitcast.8), custom_call_target="tpu_custom_call" | custom-call | bytes 6000000 | tf_op jit(solution)/shard_map/pack/pallas_call | solution.py:323
  3.5 4.6 %collective-permute-start = (bf16[24,128,128]{2,1,0:T(8,128)(2,1)S(1)}, bf16[24,128,128]{2,1,0:T(8,128)(2,1)S(1)}, u32[]{:S(2)}, u32[]{:S(2)}) collective-permute-start(bf16[24,128,128]{2,1,0:T(8,128)(2,1)S(1)} %get-tuple-element.7), channel_id=1, source_target_pairs={{4,8},{8,4},{12,16},{16,12},{20,24},{24,20},{28,32},{32,28},{36,40... | collective-permute-start | bytes 2359304 | tf_op jit(solution)/shard_map/ppermute | solution.py:296
  8.1 0.1 collective-permute-start.1
  8.2 0.0 copy-done.3
  8.2 0.0 copy-start.1
  8.2 0.0 copy-start.2
  8.2 6.7 %own_pairs.1 = (f32[24,128]{1,0:T(8,128)S(1)}, bf16[16,5,80,256]{3,2,1,0:T(8,128)(2,1)S(1)}) custom-call(bf16[6,16,128,128]{3,2,1,0:T(8,128)(2,1)S(1)} %bitcast.9, bf16[656,256]{1,0:T(8,128)(2,1)S(1)} %copy-done.3), custom_call_target="tpu_custom_call" | custom-call | flops 8000000000 | bytes 6000000 | tf_op jit(solution)/shard_map/own_pairs/pallas_call | solution.py:340
  15.0 2.8 %collective-permute-done.outer_ref = bf16[24,128,128]{2,1,0:T(8,128)(2,1)S(1)} collective-permute-done((bf16[24,128,128]{2,1,0:T(8,128)(2,1)S(1)}, bf16[24,128,128]{2,1,0:T(8,128)(2,1)S(1)}, u32[]{:S(2)}, u32[]{:S(2)}) %collective-permute-start) | collective-permute-done | bytes 786464 | tf_op jit(solution)/shard_map/ppermute | solution.py:296
  17.8 0.0 collective-permute-done.1.inner_ref
  17.8 0.0 copy-done.1
  17.8 0.0 copy-done.2
  17.8 4.5 %border_pairs.1 = f32[40,128]{1,0:T(8,128)S(1)} custom-call(s32[2]{0:T(128)S(1)} %pad_add_fusion.place_ref, bf16[24,128,128]{2,1,0:T(8,128)(2,1)S(1)} %collective-permute-done.outer_ref, bf16[24,128,128]{2,1,0:T(8,128)(2,1)S(1)} %collective-permute-done.1.inner_ref, bf16[16,5,80,256]{3,2,1,0:T(8,128)(2,1)S(1)} %get-tuple-element.10.kept_ref, ...), custom_call_target="tpu_custom_call" | custom-call | flops 4000000000 | bytes 4000000 | tf_op jit(solution)/shard_map/border_pairs/pallas_call | solution.py:360
  22.3 2.5 %collective-permute-start.4 = (f32[40,128]{1,0:T(8,128)S(1)}, f32[40,128]{1,0:T(8,128)S(1)}, u32[]{:S(2)}, u32[]{:S(2)}) collective-permute-start(f32[40,128]{1,0:T(8,128)S(1)} %border_pairs.1), channel_id=1, source_target_pairs={{0,3},{1,0},{2,1},{3,2},{4,7},{5,4},{6,5},{7,6},{8,11},{9,8},{10,9... | collective-permute-start | bytes 61448 | tf_op jit(solution)/shard_map/ppermute | solution.py:301
  24.8 0.5 collective-permute-start.3
  25.4 0.6 %collective-permute-start.2 = (f32[40,128]{1,0:T(8,128)S(1)}, f32[40,128]{1,0:T(8,128)S(1)}, u32[]{:S(2)}, u32[]{:S(2)}) collective-permute-start(f32[40,128]{1,0:T(8,128)S(1)} %border_pairs.1), channel_id=1, source_target_pairs={{0,1},{1,2},{2,3},{3,0},{4,5},{5,6},{6,7},{7,4},{8,9},{9,10},{10,1... | collective-permute-start | bytes 61448 | tf_op jit(solution)/shard_map/ppermute | solution.py:301
  26.0 0.0 collective-permute-done.4
  26.0 3.0 %collective-permute-done.3 = f32[40,128]{1,0:T(8,128)S(1)} collective-permute-done((f32[40,128]{1,0:T(8,128)S(1)}, f32[40,128]{1,0:T(8,128)S(1)}, u32[]{:S(2)}, u32[]{:S(2)}) %collective-permute-start.3) | collective-permute-done | bytes 20512 | tf_op jit(solution)/shard_map/ppermute | solution.py:301
  29.0 0.2 collective-permute-done.2
  29.2 0.1 collective-permute-start.6
  29.3 3.5 %collective-permute-start.5 = (f32[40,128]{1,0:T(8,128)S(1)}, f32[40,128]{1,0:T(8,128)S(1)}, u32[]{:S(2)}, u32[]{:S(2)}) collective-permute-start(f32[40,128]{1,0:T(8,128)S(1)} %add_add_fusion), channel_id=1, source_target_pairs={{0,4},{4,8},{8,12},{12,16},{16,20},{20,24},{24,28},{28,32},{32,36}... | collective-permute-start | bytes 61448 | tf_op jit(solution)/shard_map/ppermute | solution.py:301
  32.8 1.4 %collective-permute-done.6 = f32[40,128]{1,0:T(8,128)S(1)} collective-permute-done((f32[40,128]{1,0:T(8,128)S(1)}, f32[40,128]{1,0:T(8,128)S(1)}, u32[]{:S(2)}, u32[]{:S(2)}) %collective-permute-start.6) | collective-permute-done | bytes 20512 | tf_op jit(solution)/shard_map/ppermute | solution.py:301
  34.2 0.4 collective-permute-done.5
  34.6 8.2 %collective-permute-start.8 = (f32[3,40,128]{2,1,0:T(8,128)S(1)}, f32[3,40,128]{2,1,0:T(8,128)S(1)}, u32[]{:S(2)}, u32[]{:S(2)}) collective-permute-start(f32[3,40,128]{2,1,0:T(8,128)S(1)} %pad_maximum_fusion.near_ref), channel_id=1, source_target_pairs={{0,244},{4,248},{8,252},{12,0},{16,4},{20,8},{24,12},{28,16},{32,2... | collective-permute-start | bytes 184328 | tf_op jit(solution)/shard_map/ppermute | solution.py:301
  42.8 0.0 collective-permute-start.7
  42.8 1.8 %collective-permute-done.8.high_ref = f32[3,40,128]{2,1,0:T(8,128)S(1)} collective-permute-done((f32[3,40,128]{2,1,0:T(8,128)S(1)}, f32[3,40,128]{2,1,0:T(8,128)S(1)}, u32[]{:S(2)}, u32[]{:S(2)}) %collective-permute-start.8) | collective-permute-done | bytes 61472 | tf_op jit(solution)/shard_map/ppermute | solution.py:301
  44.6 5.2 %collective-permute-done.7.low_ref = f32[3,40,128]{2,1,0:T(8,128)S(1)} collective-permute-done((f32[3,40,128]{2,1,0:T(8,128)S(1)}, f32[3,40,128]{2,1,0:T(8,128)S(1)}, u32[]{:S(2)}, u32[]{:S(2)}) %collective-permute-start.7) | collective-permute-done | bytes 61472 | tf_op jit(solution)/shard_map/ppermute | solution.py:301
  49.8 2.1 %relax.1 = (f32[2,6,2,8]{3,2,1,0:T(2,128)}, f32[2,6,3,2,8]{4,3,2,1,0:T(2,128)}) custom-call(s32[2]{0:T(128)S(1)} %pad_add_fusion.place_ref, f32[3,40,128]{2,1,0:T(8,128)S(1)} %pad_maximum_fusion.near_ref, f32[3,40,128]{2,1,0:T(8,128)S(1)} %collective-permute-done.7.low_ref, f32[3,40,128]{2,1,0:T(8,128)S(1)} %collective-permute-done.8.high_ref), custom_call_target="tpu_custom_call" | custom-call | tf_op jit(solution)/shard_map/relax/pallas_call | solution.py:387
  (2 shorter events, 0.0 us)
Async XLA Ops:
  0.7 1.9 %copy-start = (bf16[6,2,8,128,128]{4,3,2,1,0:T(8,128)(2,1)S(1)}, bf16[6,2,8,128,128]{4,3,2,1,0:T(8,128)(2,1)}, u32[]{:S(2)}) copy-start(bf16[6,2,8,128,128]{4,3,2,1,0:T(8,128)(2,1)} %param.4) | copy-start | bytes 9437188
  2.6 5.6 %copy-start.3 = (bf16[656,256]{1,0:T(8,128)(2,1)S(1)}, bf16[656,256]{1,0:T(8,128)(2,1)}, u32[]{:S(2)}) copy-start(bf16[656,256]{1,0:T(8,128)(2,1)} %constant.11.clone.tabs_ref) | copy-start | bytes 1007620
  3.5 14.3 %collective-permute-start = (bf16[24,128,128]{2,1,0:T(8,128)(2,1)S(1)}, bf16[24,128,128]{2,1,0:T(8,128)(2,1)S(1)}, u32[]{:S(2)}, u32[]{:S(2)}) collective-permute-start(bf16[24,128,128]{2,1,0:T(8,128)(2,1)S(1)} %get-tuple-element.7), channel_id=1, source_target_pairs={{4,8},{8,4},{12,16},{16,12},{20,24},{24,20},{28,32},{32,28},{36,40... | collective-permute-start | bytes 2359304 | tf_op jit(solution)/shard_map/ppermute | solution.py:296
  8.1 9.7 %collective-permute-start.1 = (bf16[24,128,128]{2,1,0:T(8,128)(2,1)S(1)}, bf16[24,128,128]{2,1,0:T(8,128)(2,1)S(1)}, u32[]{:S(2)}, u32[]{:S(2)}) collective-permute-start(bf16[24,128,128]{2,1,0:T(8,128)(2,1)S(1)} %get-tuple-element.8), channel_id=1, source_target_pairs={{0,4},{4,0},{8,12},{12,8},{16,20},{20,16},{24,28},{28,24},{32,36},... | collective-permute-start | bytes 2359304 | tf_op jit(solution)/shard_map/ppermute | solution.py:296
  8.2 9.6 %copy-start.1 = (f32[2,6,2,8]{3,2,1,0:T(2,128)S(1)}, f32[2,6,2,8]{3,2,1,0:T(2,128)}, u32[]{:S(2)}) copy-start(f32[2,6,2,8]{3,2,1,0:T(2,128)} %nodes_ref.1) | copy-start | bytes 2308
  8.2 9.5 %copy-start.2 = (s32[6,3]{0,1:T(4,128)S(1)}, s32[6,3]{0,1:T(4,128)}, u32[]{:S(2)}) copy-start(s32[6,3]{0,1:T(4,128)} %param.5) | copy-start | bytes 220
  22.3 3.7 %collective-permute-start.4 = (f32[40,128]{1,0:T(8,128)S(1)}, f32[40,128]{1,0:T(8,128)S(1)}, u32[]{:S(2)}, u32[]{:S(2)}) collective-permute-start(f32[40,128]{1,0:T(8,128)S(1)} %border_pairs.1), channel_id=1, source_target_pairs={{0,3},{1,0},{2,1},{3,2},{4,7},{5,4},{6,5},{7,6},{8,11},{9,8},{10,9... | collective-permute-start | bytes 61448 | tf_op jit(solution)/shard_map/ppermute | solution.py:301
  24.8 4.1 %collective-permute-start.3 = (f32[40,128]{1,0:T(8,128)S(1)}, f32[40,128]{1,0:T(8,128)S(1)}, u32[]{:S(2)}, u32[]{:S(2)}) collective-permute-start(f32[40,128]{1,0:T(8,128)S(1)} %border_pairs.1), channel_id=1, source_target_pairs={{0,2},{1,3},{2,0},{3,1},{4,6},{5,7},{6,4},{7,5},{8,10},{9,11},{10,... | collective-permute-start | bytes 61448 | tf_op jit(solution)/shard_map/ppermute | solution.py:301
  25.4 3.8 %collective-permute-start.2 = (f32[40,128]{1,0:T(8,128)S(1)}, f32[40,128]{1,0:T(8,128)S(1)}, u32[]{:S(2)}, u32[]{:S(2)}) collective-permute-start(f32[40,128]{1,0:T(8,128)S(1)} %border_pairs.1), channel_id=1, source_target_pairs={{0,1},{1,2},{2,3},{3,0},{4,5},{5,6},{6,7},{7,4},{8,9},{9,10},{10,1... | collective-permute-start | bytes 61448 | tf_op jit(solution)/shard_map/ppermute | solution.py:301
  29.2 5.0 %collective-permute-start.6 = (f32[40,128]{1,0:T(8,128)S(1)}, f32[40,128]{1,0:T(8,128)S(1)}, u32[]{:S(2)}, u32[]{:S(2)}) collective-permute-start(f32[40,128]{1,0:T(8,128)S(1)} %add_add_fusion), channel_id=1, source_target_pairs={{0,252},{4,0},{8,4},{12,8},{16,12},{20,16},{24,20},{28,24},{32,28}... | collective-permute-start | bytes 61448 | tf_op jit(solution)/shard_map/ppermute | solution.py:301
  29.3 5.3 %collective-permute-start.5 = (f32[40,128]{1,0:T(8,128)S(1)}, f32[40,128]{1,0:T(8,128)S(1)}, u32[]{:S(2)}, u32[]{:S(2)}) collective-permute-start(f32[40,128]{1,0:T(8,128)S(1)} %add_add_fusion), channel_id=1, source_target_pairs={{0,4},{4,8},{8,12},{12,16},{16,20},{20,24},{24,28},{28,32},{32,36}... | collective-permute-start | bytes 61448 | tf_op jit(solution)/shard_map/ppermute | solution.py:301
  34.6 10.0 %collective-permute-start.8 = (f32[3,40,128]{2,1,0:T(8,128)S(1)}, f32[3,40,128]{2,1,0:T(8,128)S(1)}, u32[]{:S(2)}, u32[]{:S(2)}) collective-permute-start(f32[3,40,128]{2,1,0:T(8,128)S(1)} %pad_maximum_fusion.near_ref), channel_id=1, source_target_pairs={{0,244},{4,248},{8,252},{12,0},{16,4},{20,8},{24,12},{28,16},{32,2... | collective-permute-start | bytes 184328 | tf_op jit(solution)/shard_map/ppermute | solution.py:301
  42.8 7.1 %collective-permute-start.7 = (f32[3,40,128]{2,1,0:T(8,128)S(1)}, f32[3,40,128]{2,1,0:T(8,128)S(1)}, u32[]{:S(2)}, u32[]{:S(2)}) collective-permute-start(f32[3,40,128]{2,1,0:T(8,128)S(1)} %pad_maximum_fusion.near_ref), channel_id=1, source_target_pairs={{0,12},{4,16},{8,20},{12,24},{16,28},{20,32},{24,36},{28,40},{32,4... | collective-permute-start | bytes 184328 | tf_op jit(solution)/shard_map/ppermute | solution.py:301
